TPU v7x, 512 devices: a whole 4x8x8 slice. The times are simulated.
512 devices in a mesh: row: 64 (over z, x, y_hi), col: 8 (over y_lo, core).
Axes of the slice: x: 4, y: 8 (y_hi: 2, y_lo: 4; y = y_hi * 4 + y_lo), z: 8, core: 2. Of those that a mesh axis runs over, the one named last changes fastest.
Arguments:
- inputs: bfloat16 [256, 12288], P('row', 'col'), may hold values from -6 to 6
- up_weight: bfloat16 [12288, 24576], P('col', 'row'), may hold values from -0.109375 to 0.109375
- down_weight: bfloat16 [24576, 12288], P('row', 'col'), may hold values from -0.078125 to 0.078125
- out_grad: bfloat16 [256, 12288], P('row', 'col'), may hold values from -6 to 6
- block_mask: int32 [96, 192], replicated, may hold values from 0 to 1, as said below
Outputs:
- outputs: bfloat16 [256, 12288], P('row', 'col')
- in_grad: bfloat16 [256, 12288], P('row', 'col')
- up_grad: bfloat16 [12288, 24576], P('col', 'row')
- down_grad: bfloat16 [24576, 12288], P('row', 'col')
Inputs may be any that keep to these rules, and one draw needn't show every extreme that they name: `block_mask`: 1 marks a kept block: block (i, j) of up_weight and block (j, i) of down_weight; 0 marks a block that is zero. The kept blocks are the union of a butterfly pattern (rows and columns each carry a 5-bit code; block (i, j) is kept when the codes of i and j differ in at most one bit), 3 full block rows and 6 full block columns.
All inputs are finite; a program needn't handle non-finite values.
Results may differ from a plain program's by a relative error of at most 0.005.
Values may be sent and summed in bfloat16 or wider, within the bound.
No kernel may reach another device: no remote copies, remote signals or barrier semaphores. Data moves between devices by JAX's collectives and lax.ppermute only.
A program may use at most 64 MiB of HBM per device.

v0:
```python
import jax
import jax.numpy as jnp
from jax import lax
from jax.sharding import PartitionSpec as P

BLK = 128


slope_coef = 0.7978845608
cubic_coef = 0.044715


def gelu_value(values):
    tangent = jnp.tanh(slope_coef * (values + cubic_coef * values * values * values))
    return 0.5 * values * (1.0 + tangent)


def gelu_slope(values):
    tangent = jnp.tanh(slope_coef * (values + cubic_coef * values * values * values))
    return 0.5 * (1.0 + tangent) + 0.5 * values * (1.0 - tangent * tangent) * slope_coef * (
        1.0 + 3.0 * cubic_coef * values * values
    )


def apply_blocks(matrix, blocks):
    rows_b, cols_b = blocks.shape
    shaped = (
        matrix.reshape(rows_b, BLK, cols_b, BLK) * blocks.astype(matrix.dtype)[:, None, :, None]
    )
    return shaped.reshape(matrix.shape)


def local(inputs, up_weight, down_weight, out_grad, block_mask):
    row_index = lax.axis_index("row")
    col_index = lax.axis_index("col")
    d_blocks = up_weight.shape[0] // BLK
    f_blocks = up_weight.shape[1] // BLK
    local_mask = lax.dynamic_slice(
        block_mask, (col_index * d_blocks, row_index * f_blocks), (d_blocks, f_blocks)
    )
    down_mask = local_mask.T
    panel_in, panel_grad = (
        lax.all_gather(inputs, "row", axis=0, tiled=True),
        lax.all_gather(out_grad, "row", axis=0, tiled=True),
    )
    up_masked = apply_blocks(up_weight, local_mask)
    down_masked = apply_blocks(down_weight, down_mask)
    partial_value = jnp.dot(panel_in, up_masked, preferred_element_type=jnp.float32)
    hidden = lax.psum(partial_value, "col")
    full_act = gelu_value(hidden).astype(jnp.bfloat16)
    out_terms = jnp.dot(full_act, down_masked, preferred_element_type=jnp.float32)
    grad_partial = lax.dot_general(
        panel_grad, down_masked, (((1,), (1,)), ((), ())), preferred_element_type=jnp.float32
    )
    outputs = lax.psum_scatter(out_terms, "row", scatter_dimension=0, tiled=True).astype(
        jnp.bfloat16
    )
    grad_hidden = lax.psum(grad_partial, "col")
    full_dact = (grad_hidden * gelu_slope(hidden)).astype(jnp.bfloat16)
    down_full = lax.dot_general(
        full_act, panel_grad, (((0,), (0,)), ((), ())), preferred_element_type=jnp.float32
    )
    down_grad = apply_blocks(down_full, down_mask).astype(jnp.bfloat16)
    up_full = lax.dot_general(
        panel_in, full_dact, (((0,), (0,)), ((), ())), preferred_element_type=jnp.float32
    )
    up_grad = apply_blocks(up_full, local_mask).astype(jnp.bfloat16)
    in_terms = lax.dot_general(
        full_dact, up_masked, (((1,), (1,)), ((), ())), preferred_element_type=jnp.float32
    )
    in_grad = lax.psum_scatter(in_terms, "row", scatter_dimension=0, tiled=True).astype(
        jnp.bfloat16
    )
    return (outputs, in_grad, up_grad, down_grad)


def solution(mesh):
    in_specs = (P("row", "col"), P("col", "row"), P("row", "col"), P("row", "col"), P())
    out_specs = (P("row", "col"), P("row", "col"), P("col", "row"), P("row", "col"))
    return jax.shard_map(local, mesh=mesh, in_specs=in_specs, out_specs=out_specs, check_vma=False)
```

profile of v0, /device:TPU:48, one launch (start us, length us, event | category | flops | bytes accessed | tf_op | source)
XLA Modules:
  0.0 1100.9 jit_solution(739576390966212849)
XLA Ops:
  7.2 0.8 dynamic-slice_convert_fusion.2
  8.3 229.0 %all-gather = bf16[64,4,1536]{2,1,0:T(4,128)(2,1)S(1)} all-gather(bf16[1,4,1536]{2,1,0:T(4,128)(2,1)} %bitcast.53), channel_id=1, replica_groups=mesh['row'=64,'col'=8] {'row'}, dimensions={0}, use_global_device_ids=true | all-gather | bytes 798720 | tf_op jit(solution)/shard_map/all_gather | solution.py:43
  237.3 0.2 reshape.25
  237.5 225.6 %all-gather.1 = bf16[64,4,1536]{2,1,0:T(4,128)(2,1)S(1)} all-gather(bf16[1,4,1536]{2,1,0:T(4,128)(2,1)S(1)} %bitcast.54), channel_id=1, replica_groups=mesh['row'=64,'col'=8] {'row'}, dimensions={0}, use_global_device_ids=true | all-gather | bytes 798720 | tf_op jit(solution)/shard_map/all_gather | solution.py:44
  463.2 1.9 copy.20
  465.1 0.3 mul.102
  465.4 1.4 convolution_bitcast_fusion.2
  466.8 0.3 mul.111
  467.1 1.0 copy-done.9
  468.0 1.3 convolution_bitcast_fusion.1
  469.5 1.3 dynamic-slice
  471.5 64.9 %all-reduce.7.cloned.1.call-done = (f32[256,384]{0,1:T(8,128)}, f32[256,384]{0,1:T(8,128)}) async-done(((f32[256,384]{0,1:T(8,128)}, f32[256,384]{0,1:T(8,128)}), (f32[256,384]{0,1:T(8,128)}, f32[256,384]{0,1:T(8,128)})) %all-reduce.7.cloned.1.call-update) | async-done | bytes 786448 | tf_op jit(solution)/shard_map/psum | solution.py:49
  536.4 2.2 fusion.11
  538.6 0.3 fusion.9
  538.9 0.6 fusion.10
  539.5 0.3 mul.123
  539.8 0.8 copy-done.8
  540.6 1.9 fusion.1
  542.5 2.4 copy.24
  544.9 0.3 mul.126
  545.2 0.9 copy-done.6
  546.0 2.0 fusion.2
  548.0 544.7 %all-reduce.8 = (bf16[256,1536]{1,0:T(8,128)(2,1)}, bf16[256,1536]{1,0:T(8,128)(2,1)}) all-reduce(f32[256,1536]{1,0:T(8,128)S(1)} %fusion.11, f32[256,1536]{1,0:T(8,128)S(1)} %fusion.10), channel_id=2, replica_groups=mesh['row'=64,'col'=8] {'row'}, use_global_device_ids=true, to_apply=%region_1.0.clone | all-reduce | flops 786432 | bytes 4718592
  1092.7 1.4 dynamic-slice_convert_fusion
  (28 shorter events, 0.7 us)
Async XLA Ops:
  7.2 529.2 %all-reduce.7.cloned.1.call-start = ((), (), s32[]{:S(2)}) async-start(), calls=%async_computation | async-start | bytes 1572864 | tf_op jit(solution)/shard_map/psum | solution.py:49
  8.3 229.2 %copy-start.11 = (bf16[4,1536]{1,0:T(4,128)(2,1)S(1)}, bf16[4,1536]{1,0:T(4,128)(2,1)}, u32[]{:S(2)}) copy-start(bf16[4,1536]{1,0:T(4,128)(2,1)} %param.8) | copy-start | bytes 36868
  237.5 227.9 %copy-start.7 = (bf16[256,1536]{1,0:T(8,128)(2,1)}, bf16[256,1536]{1,0:T(8,128)(2,1)S(1)}, u32[]{:S(2)}) copy-start(bf16[256,1536]{1,0:T(8,128)(2,1)S(1)} %reshape.25) | copy-start | bytes 2359300
  463.2 3.8 copy-start.5
  465.1 1.7 copy-start.2
  465.4 1.4 copy-start
  466.8 1.3 copy-start.9
  536.3 2.3 copy-start.4
  536.4 2.3 copy-start.10
  536.4 2.5 copy-start.1
  536.4 2.5 copy-start.3
  539.5 1.1 copy-start.8
  544.9 1.1 copy-start.6
Sparse Core Ops, SparseCore 0:
  469.5 66.8 all-reduce.6
where the time goes:
time: 1100 us
  blocking collectives  999 us (91%)
  waiting for transfers between devices  64.9 us (6%)
  between operations  14.9 us (1%)
  local copies, waits for them, and re-layouts  11.4 us (1%)
    unnamed x1, blocking collectives  545 us
    all_gather x1, blocking collectives, local(): lax.all_gather(inputs, 'row', axis=0, tiled=True)  229 us
    all_gather x1, blocking collectives, local(): lax.all_gather(out_grad, 'row', axis=0, tiled=True)  226 us
    psum x1, waiting for transfers between devices, local(): hidden = lax.psum(partial_value, 'col')  64.9 us
  transfers between devices with their start and end apart: 1, of which 1 were waited for; matrix products, arithmetic and copies ran while one was open for 0% of the time, Pallas kernels for 0%

commit v1 on v0

v1 whole, which is shorter than its diff:
```python
import jax
import jax.numpy as jnp
from jax import lax
from jax.sharding import Mesh, PartitionSpec as P

BLK = 128
AXES = ("zh", "zl", "x", "yh", "yl", "core")
SIZES = (4, 2, 4, 2, 4, 2)
ROW = ("zh", "zl", "x", "yh")
COL = ("yl", "core")
FAR = ("zh", "yh")
NEAR = ("x", "zl")

slope_coef = 0.7978845608
cubic_coef = 0.044715


def gelu_pair(values):
    tangent = jnp.tanh(slope_coef * (values + cubic_coef * values * values * values))
    value = 0.5 * values * (1.0 + tangent)
    slope = 0.5 * (1.0 + tangent) + 0.5 * values * (1.0 - tangent * tangent) * slope_coef * (
        1.0 + 3.0 * cubic_coef * values * values
    )
    return value, slope


def apply_blocks(matrix, blocks):
    rows_b, cols_b = blocks.shape
    shaped = (
        matrix.reshape(rows_b, BLK, cols_b, BLK) * blocks.astype(matrix.dtype)[:, None, :, None]
    )
    return shaped.reshape(matrix.shape)


def spread(block, axes, count):
    copies = jnp.broadcast_to(block[None], (count,) + block.shape)
    return lax.all_to_all(copies, axes, split_axis=0, concat_axis=0, tiled=True)


def swap(blocks, axes):
    return lax.all_to_all(blocks, axes, split_axis=0, concat_axis=0, tiled=True)


def local(inputs, up_weight, down_weight, out_grad, block_mask):
    row_index = lax.axis_index(ROW)
    col_index = lax.axis_index(COL)
    core = lax.axis_index("core")
    rows, width = inputs.shape
    units = up_weight.shape[1]
    d_blocks = width // BLK
    f_blocks = units // BLK
    local_mask = lax.dynamic_slice(
        block_mask, (col_index * d_blocks, row_index * f_blocks), (d_blocks, f_blocks)
    )
    down_mask = local_mask.T
    up_masked = apply_blocks(up_weight, local_mask)
    down_masked = apply_blocks(down_weight, down_mask)

    both = jnp.stack([inputs, out_grad])
    far = spread(both, FAR, 8)
    far = far.transpose(1, 0, 2, 3).reshape(2, 8 * rows, width)
    near = spread(far, NEAR, 8)
    tokens = 64 * rows
    panel_in = near[:, 0].reshape(tokens, width)
    panel_grad = near[:, 1].reshape(tokens, width)

    part_hidden = jnp.dot(panel_in, up_masked, preferred_element_type=jnp.float32)
    part_grad = lax.dot_general(
        panel_grad, down_masked, (((1,), (1,)), ((), ())), preferred_element_type=jnp.float32
    )
    half = tokens // 2
    parts = jnp.stack([part_hidden, part_grad]).reshape(2, 2, half, units)
    keep = jnp.where(core == 0, parts[:, 0], parts[:, 1])
    give = jnp.where(core == 0, parts[:, 1], parts[:, 0]).astype(jnp.bfloat16)
    got = lax.ppermute(give, "core", [(0, 1), (1, 0)])
    pair = (keep + got.astype(jnp.float32)).astype(jnp.bfloat16)
    quarter = half // 4
    pair = pair.reshape(2, 4, quarter, units).transpose(1, 0, 2, 3)
    summed = jnp.sum(swap(pair, "yl").astype(jnp.float32), axis=0)
    value, slope = gelu_pair(summed[0])
    acts = jnp.stack([value, summed[1] * slope]).astype(jnp.bfloat16)
    acts = spread(acts, "yl", 4)
    acts = acts.transpose(1, 0, 2, 3).reshape(1, 2, half, units)
    acts = lax.all_gather(acts, "core", axis=0, tiled=True)
    full_act = acts[:, 0].reshape(tokens, units)
    full_dact = acts[:, 1].reshape(tokens, units)

    out_terms = jnp.dot(full_act, down_masked, preferred_element_type=jnp.float32)
    in_terms = lax.dot_general(
        full_dact, up_masked, (((1,), (1,)), ((), ())), preferred_element_type=jnp.float32
    )
    down_full = lax.dot_general(
        full_act, panel_grad, (((0,), (0,)), ((), ())), preferred_element_type=jnp.float32
    )
    down_grad = apply_blocks(down_full, down_mask).astype(jnp.bfloat16)
    up_full = lax.dot_general(
        panel_in, full_dact, (((0,), (0,)), ((), ())), preferred_element_type=jnp.float32
    )
    up_grad = apply_blocks(up_full, local_mask).astype(jnp.bfloat16)

    terms = jnp.stack([out_terms, in_terms]).astype(jnp.bfloat16)
    terms = terms.reshape(2, 8, 8 * rows, width).transpose(1, 0, 2, 3)
    sums = jnp.sum(swap(terms, NEAR).astype(jnp.float32), axis=0).astype(jnp.bfloat16)
    sums = sums.reshape(2, 8, rows, width).transpose(1, 0, 2, 3)
    totals = jnp.sum(swap(sums, FAR).astype(jnp.float32), axis=0).astype(jnp.bfloat16)
    return (totals[0], totals[1], up_grad, down_grad)


def solution(mesh):
    fine = Mesh(mesh.devices.reshape(SIZES), AXES)
    in_specs = (P(ROW, COL), P(COL, ROW), P(ROW, COL), P(ROW, COL), P())
    out_specs = (P(ROW, COL), P(ROW, COL), P(COL, ROW), P(ROW, COL))
    return jax.shard_map(local, mesh=fine, in_specs=in_specs, out_specs=out_specs, check_vma=False)
```

time: 1100 us -> 136 us (0.12)
  the two profiles are of different devices: /device:TPU:48 before, /device:TPU:1 now
where the time goes in v1:
time: 136 us
  blocking collectives  52 us (38%)
  waiting for transfers between devices  42.6 us (31%)
  starting transfers between devices  17.2 us (13%)
  local copies, waits for them, and re-layouts  16.5 us (12%)
  matrix products  3.57 us (3%)
  other arithmetic  2.92 us (2%)
    all_to_all x2, blocking collectives, spread(): return lax.all_to_all(copies, axes, split_axis=0, concat_axis=0, tiled=True)  37.9 us
    all_to_all x2, waiting for transfers between devices, swap(): return lax.all_to_all(blocks, axes, split_axis=0, concat_axis=0, tiled=True)  25.2 us
    all_to_all x1, waiting for transfers between devices, spread(): return lax.all_to_all(copies, axes, split_axis=0, concat_axis=0, tiled=True)  16.3 us
    all_to_all x1, blocking collectives, swap(): return lax.all_to_all(blocks, axes, split_axis=0, concat_axis=0, tiled=True)  9.49 us
    all_to_all x2, starting transfers between devices, swap(): return lax.all_to_all(blocks, axes, split_axis=0, concat_axis=0, tiled=True)  7.34 us
    unnamed x14, local copies, waits for them, and re-layouts  6.69 us
    ppermute x1, starting transfers between devices, local(): got = lax.ppermute(give, 'core', [(0, 1), (1, 0)])  5.26 us
    all_gather x1, blocking collectives, local(): acts = lax.all_gather(acts, 'core', axis=0, tiled=True)  4.59 us
  transfers between devices with their start and end apart: 4, of which 4 were waited for; matrix products, arithmetic and copies ran while one was open for 8% of the time, Pallas kernels for 0%

profile of v1, /device:TPU:1, one launch (start us, length us, event | category | flops | bytes accessed | tf_op | source)
XLA Modules:
  0.0 135.6 jit_solution(4918992450316282614)
XLA Ops:
  1.4 28.4 %all_to_all.30 = bf16[8,2,4,1536]{3,2,1,0:T(4,128)(2,1)S(1)} all-to-all(bf16[8,2,4,1536]{3,2,1,0:T(4,128)(2,1)S(1)} %broadcast_in_dim.8), channel_id=1, replica_groups=mesh['zh'=4,'zl'=2,'x'=4,'yh'=2,'yl'=4,'core'=2] {'zh','yh'}, dimensions={0} | all-to-all | bytes 393216 | tf_op jit(solution)/shard_map/all_to_all | solution.py:37
  30.0 1.3 broadcast_in_dim.10
  31.3 4.6 %all-to-all-start.1 = ((bf16[8,2,32,1536]{3,2,1,0:T(8,128)(2,1)}), bf16[8,2,32,1536]{3,2,1,0:T(8,128)(2,1)S(1)}, u32[]{:S(2)}, u32[]{:S(2)}) async-start(bf16[8,2,32,1536]{3,2,1,0:T(8,128)(2,1)} %broadcast_in_dim.10), calls=%async_computation.1 | async-start | bytes 3145728 | tf_op jit(solution)/shard_map/all_to_all | solution.py:37
  36.9 1.6 %copy.81 = bf16[1536,384]{0,1:T(8,128)(2,1)S(1)} copy(bf16[1536,384]{1,0:T(8,128)(2,1)} %param.6) | data formatting | bytes 2359296 | tf_op args[1]
  38.5 16.3 %all-to-all-done.1 = bf16[8,2,32,1536]{3,2,1,0:T(8,128)(2,1)S(1)} async-done(((bf16[8,2,32,1536]{3,2,1,0:T(8,128)(2,1)}), bf16[8,2,32,1536]{3,2,1,0:T(8,128)(2,1)S(1)}, u32[]{:S(2)}, u32[]{:S(2)}) %all-to-all-start.1) | async-done | bytes 1572896 | tf_op jit(solution)/shard_map/all_to_all | solution.py:37
  55.2 1.5 %copy-done.3 = bf16[384,1536]{1,0:T(8,128)(2,1)S(1)} copy-done((bf16[384,1536]{1,0:T(8,128)(2,1)S(1)}, bf16[384,1536]{1,0:T(8,128)(2,1)}, u32[]{:S(2)}) %copy-start.3) | copy-done | bytes 1179672
  58.4 5.3 %collective-permute-start = (bf16[2,128,384]{2,1,0:T(8,128)(2,1)S(1)}, bf16[2,128,384]{2,1,0:T(8,128)(2,1)S(1)}, u32[]{:S(2)}, u32[]{:S(2)}) collective-permute-start(bf16[2,128,384]{2,1,0:T(8,128)(2,1)S(1)} %fusion.8), channel_id=1, source_target_pairs={{0,1},{1,0},{2,3},{3,2},{4,5},{5,4},{6,7},{7,6},{8,9},{9,8},{10,11... | collective-permute-start | bytes 589832 | tf_op jit(solution)/shard_map/ppermute | solution.py:75
  63.7 1.0 collective-permute-done
  64.8 9.5 %all_to_all.31 = bf16[4,2,32,384]{3,2,1,0:T(8,128)(2,1)S(1)} all-to-all(bf16[4,2,32,384]{3,2,1,0:T(8,128)(2,1)S(1)} %bitcast.153), channel_id=1, replica_groups=mesh['zh'=4,'zl'=2,'x'=4,'yh'=2,'yl'=4,'core'=2] {'yl'}, dimensions={0} | all-to-all | bytes 393216 | tf_op jit(solution)/shard_map/all_to_all | solution.py:41
  74.4 9.5 %all_to_all.32 = bf16[4,2,32,384]{3,2,1,0:T(8,128)(2,1)S(1)} all-to-all(bf16[4,2,32,384]{3,2,1,0:T(8,128)(2,1)S(1)} %broadcast_in_dim.11), channel_id=1, replica_groups=mesh['zh'=4,'zl'=2,'x'=4,'yh'=2,'yl'=4,'core'=2] {'yl'}, dimensions={0} | all-to-all | bytes 393216 | tf_op jit(solution)/shard_map/all_to_all | solution.py:37
  84.0 4.6 %all_gather.3 = bf16[2,2,128,384]{3,2,1,0:T(8,128)(2,1)S(1)} all-gather(bf16[1,2,128,384]{3,2,1,0:T(8,128)(2,1)S(1)} %bitcast.155), channel_id=1, replica_groups=mesh['zh'=4,'zl'=2,'x'=4,'yh'=2,'yl'=4,'core'=2] {'core'}, dimensions={0}, use_global_device_ids=true | all-gather | bytes 589824 | tf_op jit(solution)/shard_map/all_gather | solution.py:84
  90.0 1.3 copy.91
  91.2 3.7 %all-to-all-start.4 = ((bf16[8,2,32,1536]{3,2,1,0:T(8,128)(2,1)}), bf16[8,2,32,1536]{3,2,1,0:T(8,128)(2,1)S(1)}, u32[]{:S(2)}, u32[]{:S(2)}) async-start(bf16[8,2,32,1536]{3,2,1,0:T(8,128)(2,1)} %copy.91), calls=%async_computation.4 | async-start | bytes 3145728 | tf_op jit(solution)/shard_map/all_to_all | solution.py:41
  95.3 1.4 %copy.98 = bf16[256,1536]{0,1:T(8,128)(2,1)S(1)} copy(bf16[256,1536]{1,0:T(8,128)(2,1)} %bitcast.140) | data formatting | bytes 1572864 | tf_op jit(solution)/shard_map/reshape;squeeze | solution.py:65
  96.7 0.8 copy.95
  97.6 18.4 %all-to-all-done.4 = bf16[8,2,32,1536]{3,2,1,0:T(8,128)(2,1)S(1)} async-done(((bf16[8,2,32,1536]{3,2,1,0:T(8,128)(2,1)}), bf16[8,2,32,1536]{3,2,1,0:T(8,128)(2,1)S(1)}, u32[]{:S(2)}, u32[]{:S(2)}) %all-to-all-start.4) | async-done | bytes 1572896 | tf_op jit(solution)/shard_map/all_to_all | solution.py:41
  116.0 0.9 reduce_sum.34
  116.9 1.1 copy.92
  118.8 3.6 %all-to-all-start.5 = ((bf16[8,2,4,1536]{3,2,1,0:T(4,128)(2,1)}), bf16[8,2,4,1536]{3,2,1,0:T(4,128)(2,1)S(1)}, u32[]{:S(2)}, u32[]{:S(2)}) async-start(bf16[8,2,4,1536]{3,2,1,0:T(4,128)(2,1)} %copy.93), calls=%async_computation.5 | async-start | bytes 393216 | tf_op jit(solution)/shard_map/all_to_all | solution.py:41
  123.1 1.0 copy.108
  124.1 1.2 copy.125
  126.0 0.8 copy.100
  126.8 1.3 copy.124
  128.1 6.8 %all-to-all-done.5 = bf16[8,2,4,1536]{3,2,1,0:T(4,128)(2,1)S(1)} async-done(((bf16[8,2,4,1536]{3,2,1,0:T(4,128)(2,1)}), bf16[8,2,4,1536]{3,2,1,0:T(4,128)(2,1)S(1)}, u32[]{:S(2)}, u32[]{:S(2)}) %all-to-all-start.5) | async-done | bytes 196640 | tf_op jit(solution)/shard_map/all_to_all | solution.py:41
  (41 shorter events, 8.6 us)
Async XLA Ops:
  31.3 23.5 %all-to-all-start.1 = ((bf16[8,2,32,1536]{3,2,1,0:T(8,128)(2,1)}), bf16[8,2,32,1536]{3,2,1,0:T(8,128)(2,1)S(1)}, u32[]{:S(2)}, u32[]{:S(2)}) async-start(bf16[8,2,32,1536]{3,2,1,0:T(8,128)(2,1)} %broadcast_in_dim.10), calls=%async_computation.1 | async-start | bytes 3145728 | tf_op jit(solution)/shard_map/all_to_all | solution.py:37
  54.9 2.5 %copy-start = (bf16[8,1,32,1536]{3,2,1,0:T(8,128)(2,1)}, bf16[8,1,32,1536]{3,2,1,0:T(8,128)(2,1)S(1)}, u32[]{:S(2)}) copy-start(bf16[8,1,32,1536]{3,2,1,0:T(8,128)(2,1)S(1)} %get-tuple-element.21) | copy-start | bytes 2359300
  54.9 2.8 %copy-start.1 = (bf16[8,1,32,1536]{3,2,1,0:T(8,128)(2,1)}, bf16[8,1,32,1536]{3,2,1,0:T(8,128)(2,1)S(1)}, u32[]{:S(2)}) copy-start(bf16[8,1,32,1536]{3,2,1,0:T(8,128)(2,1)S(1)} %get-tuple-element.20) | copy-start | bytes 2359300
  54.9 1.8 %copy-start.3 = (bf16[384,1536]{1,0:T(8,128)(2,1)S(1)}, bf16[384,1536]{1,0:T(8,128)(2,1)}, u32[]{:S(2)}) copy-start(bf16[384,1536]{1,0:T(8,128)(2,1)} %param.7) | copy-start | bytes 3538948
  58.4 6.3 %collective-permute-start = (bf16[2,128,384]{2,1,0:T(8,128)(2,1)S(1)}, bf16[2,128,384]{2,1,0:T(8,128)(2,1)S(1)}, u32[]{:S(2)}, u32[]{:S(2)}) collective-permute-start(bf16[2,128,384]{2,1,0:T(8,128)(2,1)S(1)} %fusion.8), channel_id=1, source_target_pairs={{0,1},{1,0},{2,3},{3,2},{4,5},{5,4},{6,7},{7,6},{8,9},{9,8},{10,11... | collective-permute-start | bytes 589832 | tf_op jit(solution)/shard_map/ppermute | solution.py:75
  91.2 3.8 %copy-start.2 = (bf16[8,1,32,1536]{3,2,1,0:T(8,128)(2,1)S(1)}, bf16[8,1,32,1536]{3,2,1,0:T(8,128)(2,1)}, u32[]{:S(2)}) copy-start(bf16[8,1,32,1536]{3,2,1,0:T(8,128)(2,1)} %copy-done.1) | copy-start | bytes 2359300
  91.2 24.8 %all-to-all-start.4 = ((bf16[8,2,32,1536]{3,2,1,0:T(8,128)(2,1)}), bf16[8,2,32,1536]{3,2,1,0:T(8,128)(2,1)S(1)}, u32[]{:S(2)}, u32[]{:S(2)}) async-start(bf16[8,2,32,1536]{3,2,1,0:T(8,128)(2,1)} %copy.91), calls=%async_computation.4 | async-start | bytes 3145728 | tf_op jit(solution)/shard_map/all_to_all | solution.py:41
  97.6 24.9 %copy-start.4 = (bf16[256,384]{0,1:T(8,128)(2,1)S(1)}, bf16[256,384]{0,1:T(8,128)(2,1)}, u32[]{:S(2)}) copy-start(bf16[256,384]{0,1:T(8,128)(2,1)} %copy.95) | copy-start | bytes 589828
  118.8 16.1 %all-to-all-start.5 = ((bf16[8,2,4,1536]{3,2,1,0:T(4,128)(2,1)}), bf16[8,2,4,1536]{3,2,1,0:T(4,128)(2,1)S(1)}, u32[]{:S(2)}, u32[]{:S(2)}) async-start(bf16[8,2,4,1536]{3,2,1,0:T(4,128)(2,1)} %copy.93), calls=%async_computation.5 | async-start | bytes 393216 | tf_op jit(solution)/shard_map/all_to_all | solution.py:41

commit v2 on v1

v2 whole, which is shorter than its diff:
```python
import jax
import jax.numpy as jnp
from jax import lax
from jax.experimental import pallas as pl
from jax.experimental.pallas import tpu as pltpu
from jax.sharding import Mesh, PartitionSpec as P

BLK = 128
AXES = ("zh", "zl", "x", "yh", "yl", "core")
SIZES = (4, 2, 4, 2, 4, 2)
ROW = ("zh", "zl", "x", "yh")
COL = ("yl", "core")
FAR = ("zh", "yh")
NEAR = ("x", "zl")
STEPS = 3

slope_coef = 0.7978845608
cubic_coef = 0.044715


def gelu_pair(values):
    tangent = jnp.tanh(slope_coef * (values + cubic_coef * values * values * values))
    value = 0.5 * values * (1.0 + tangent)
    slope = 0.5 * (1.0 + tangent) + 0.5 * values * (1.0 - tangent * tangent) * slope_coef * (
        1.0 + 3.0 * cubic_coef * values * values
    )
    return value, slope


def spread(block, axes, count):
    copies = jnp.broadcast_to(block[None], (count,) + block.shape)
    return lax.all_to_all(copies, axes, split_axis=0, concat_axis=0, tiled=True)


def swap(blocks, axes):
    return lax.all_to_all(blocks, axes, split_axis=0, concat_axis=0, tiled=True)


def kept(mask_ref, d_block, f_block, block):
    return jnp.where(mask_ref[d_block, f_block] != 0, block, jnp.zeros_like(block))


def mask_weights(step, mask_ref, up_ref, down_ref, um, dm):
    wide, units = um.shape
    for i in range(wide // BLK):
        d = slice(i * BLK, (i + 1) * BLK)
        for j in range(units // BLK):
            f = slice(j * BLK, (j + 1) * BLK)
            d_block = step * (wide // BLK) + i
            um[d, f] = kept(mask_ref, d_block, j, up_ref[d, f])
            dm[f, d] = kept(mask_ref, d_block, j, down_ref[f, d])


def first_kernel(core_ref, mask_ref, near_ref, up_ref, down_ref, keep_ref, give_ref, um, dm, hid, grd):
    step = pl.program_id(0)
    mask_weights(step, mask_ref, up_ref, down_ref, um, dm)
    tokens, wide = hid.shape[0], um.shape[0]
    x = near_ref[:, 0].reshape(tokens, wide)
    g = near_ref[:, 1].reshape(tokens, wide)
    h = jnp.dot(x, um[...], preferred_element_type=jnp.float32)
    q = lax.dot_general(g, dm[...], (((1,), (1,)), ((), ())), preferred_element_type=jnp.float32)

    @pl.when(step == 0)
    def _():
        hid[...] = h
        grd[...] = q

    @pl.when(step > 0)
    def _():
        hid[...] += h
        grd[...] += q

    @pl.when(step == pl.num_programs(0) - 1)
    def _():
        half = tokens // 2
        low = core_ref[0] == 0
        for k, acc in enumerate((hid, grd)):
            a, b = acc[:half], acc[half:]
            keep_ref[k] = jnp.where(low, a, b)
            give_ref[k] = jnp.where(low, b, a).astype(give_ref.dtype)


def second_kernel(mask_ref, acts_ref, up_ref, down_ref, terms_ref, um, dm):
    step = pl.program_id(0)
    mask_weights(step, mask_ref, up_ref, down_ref, um, dm)
    blocks, _, rows, units = acts_ref.shape
    wide = um.shape[0]
    act = acts_ref[:, 0].reshape(blocks * rows, units)
    dact = acts_ref[:, 1].reshape(blocks * rows, units)
    out = jnp.dot(act, dm[...], preferred_element_type=jnp.float32)
    terms_ref[:, 0] = out.astype(terms_ref.dtype).reshape(blocks, rows, wide)
    back = lax.dot_general(dact, um[...], (((1,), (1,)), ((), ())), preferred_element_type=jnp.float32)
    terms_ref[:, 1] = back.astype(terms_ref.dtype).reshape(blocks, rows, wide)


def third_kernel(mask_ref, acts_ref, near_ref, upg_ref, downg_ref):
    step = pl.program_id(0)
    blocks, _, rows, units = acts_ref.shape
    wide = upg_ref.shape[0]
    tokens = blocks * rows
    act = acts_ref[:, 0].reshape(tokens, units)
    dact = acts_ref[:, 1].reshape(tokens, units)
    x = near_ref[:, 0].reshape(tokens, wide)
    g = near_ref[:, 1].reshape(tokens, wide)
    lead = (((0,), (0,)), ((), ()))
    down = lax.dot_general(act, g, lead, preferred_element_type=jnp.float32).astype(downg_ref.dtype)
    up = lax.dot_general(x, dact, lead, preferred_element_type=jnp.float32).astype(upg_ref.dtype)
    for i in range(wide // BLK):
        d = slice(i * BLK, (i + 1) * BLK)
        for j in range(units // BLK):
            f = slice(j * BLK, (j + 1) * BLK)
            d_block = step * (wide // BLK) + i
            upg_ref[d, f] = kept(mask_ref, d_block, j, up[d, f])
            downg_ref[f, d] = kept(mask_ref, d_block, j, down[f, d])


def local(inputs, up_weight, down_weight, out_grad, block_mask):
    row_index = lax.axis_index(ROW)
    col_index = lax.axis_index(COL)
    core = lax.axis_index("core")
    rows, width = inputs.shape
    units = up_weight.shape[1]
    d_blocks = width // BLK
    f_blocks = units // BLK
    tokens = 64 * rows
    half = tokens // 2
    quarter = half // 4
    wide = width // STEPS
    bf, f4 = jnp.bfloat16, jnp.float32
    smem = pl.BlockSpec(memory_space=pltpu.SMEM)
    near_spec = pl.BlockSpec((8, 2, 8 * rows, wide), lambda k: (0, 0, 0, k))
    acts_spec = pl.BlockSpec((8, 2, quarter, units), lambda k: (0, 0, 0, 0))
    up_spec = pl.BlockSpec((wide, units), lambda k: (k, 0))
    down_spec = pl.BlockSpec((units, wide), lambda k: (0, k))
    half_spec = pl.BlockSpec((2, half, units), lambda k: (0, 0, 0))
    masked = [pltpu.VMEM((wide, units), bf), pltpu.VMEM((units, wide), bf)]
    flops = 2 * 2 * tokens * width * units
    weight_bytes = 2 * 2 * width * units
    panel_bytes = 2 * 2 * tokens * width

    mask = lax.dynamic_slice(
        block_mask, (col_index * d_blocks, row_index * f_blocks), (d_blocks, f_blocks)
    )

    both = jnp.stack([inputs, out_grad])
    far = spread(both, FAR, 8)
    far, mask = lax.optimization_barrier((far, mask))
    far = far.transpose(1, 0, 2, 3).reshape(2, 8 * rows, width)
    near = spread(far, NEAR, 8)

    keep, give = pl.pallas_call(
        first_kernel,
        grid=(STEPS,),
        in_specs=[smem, smem, near_spec, up_spec, down_spec],
        out_specs=[half_spec, half_spec],
        out_shape=[
            jax.ShapeDtypeStruct((2, half, units), f4),
            jax.ShapeDtypeStruct((2, half, units), f4),
        ],
        scratch_shapes=masked + [pltpu.VMEM((tokens, units), f4)] * 2,
        cost_estimate=pl.CostEstimate(
            flops=flops, bytes_accessed=weight_bytes + panel_bytes, transcendentals=0
        ),
        name="partial_sums",
    )(core.reshape(1), mask, near, up_weight, down_weight)
    got = lax.ppermute(give, "core", [(0, 1), (1, 0)])
    pair = (keep + got).reshape(2, 4, quarter, units).transpose(1, 0, 2, 3)
    summed = jnp.sum(swap(pair, "yl"), axis=0)
    value, slope = gelu_pair(summed[0])
    acts = jnp.stack([value, summed[1] * slope]).astype(bf)
    acts = spread(acts, "yl", 4)
    acts = acts.reshape(1, 8 * quarter, units)
    acts = lax.all_gather(acts, "core", axis=0, tiled=True).reshape(8, 2, quarter, units)

    terms = pl.pallas_call(
        second_kernel,
        grid=(STEPS,),
        in_specs=[smem, acts_spec, up_spec, down_spec],
        out_specs=near_spec,
        out_shape=jax.ShapeDtypeStruct((8, 2, 8 * rows, width), bf),
        scratch_shapes=masked,
        cost_estimate=pl.CostEstimate(
            flops=flops, bytes_accessed=weight_bytes + panel_bytes, transcendentals=0
        ),
        name="output_terms",
    )(mask, acts, up_weight, down_weight)

    terms = swap(terms, NEAR)
    terms, acts, near = lax.optimization_barrier((terms, acts, near))
    sums = jnp.sum(terms.astype(f4), axis=0).astype(bf)
    sums = sums.reshape(2, 8, rows, width).transpose(1, 0, 2, 3)
    sums = swap(sums, FAR)
    up_grad, down_grad = pl.pallas_call(
        third_kernel,
        grid=(STEPS,),
        in_specs=[smem, acts_spec, near_spec],
        out_specs=[up_spec, down_spec],
        out_shape=[
            jax.ShapeDtypeStruct((width, units), bf),
            jax.ShapeDtypeStruct((units, width), bf),
        ],
        cost_estimate=pl.CostEstimate(
            flops=flops, bytes_accessed=weight_bytes + panel_bytes, transcendentals=0
        ),
        name="weight_grads",
    )(mask, acts, near)
    sums, up_grad, down_grad = lax.optimization_barrier((sums, up_grad, down_grad))
    totals = jnp.sum(sums.astype(f4), axis=0).astype(bf)
    return (totals[0], totals[1], up_grad, down_grad)


def solution(mesh):
    fine = Mesh(mesh.devices.reshape(SIZES), AXES)
    in_specs = (P(ROW, COL), P(COL, ROW), P(ROW, COL), P(ROW, COL), P())
    out_specs = (P(ROW, COL), P(ROW, COL), P(COL, ROW), P(ROW, COL))
    return jax.shard_map(local, mesh=fine, in_specs=in_specs, out_specs=out_specs, check_vma=False)
```

time: 136 us -> 143 us (1.051)
  blocking collectives: 52 us -> 75.7 us
  waiting for transfers between devices: 42.6 us -> 21 us
  Pallas kernels: 0 us -> 13.1 us
  local copies, waits for them, and re-layouts: 16.5 us -> 4.09 us
  starting transfers between devices: 17.2 us -> 25.1 us
  matrix products: 3.57 us -> 0 us
    all_to_all x1 -> x2, blocking collectives: 9.49 us -> 39.1 us  [swap(): return lax.all_to_all(blocks, axes, split_axis=0, concat_axis=0, tiled=True)]
    all_to_all x2 -> x1, waiting for transfers between devices: 25.2 us -> 8.4 us  [swap(): return lax.all_to_all(blocks, axes, split_axis=0, concat_axis=0, tiled=True)]
    pallas_call x0 -> x3, Pallas kernels: none -> 13.1 us  [the longest x1 4.61 us: local(): pl.pallas_call(first_kernel, grid=(STEPS,), in_specs=[smem, smem, near_sp...]
    all_to_all x1, starting transfers between devices: 4.56 us -> 16.1 us  [spread(): return lax.all_to_all(copies, axes, split_axis=0, concat_axis=0, tiled=True)]
    unnamed x14 -> x0, local copies, waits for them, and re-layouts: 6.69 us -> none
    all_to_all x2, blocking collectives: 37.9 us -> 31.9 us  [spread(): return lax.all_to_all(copies, axes, split_axis=0, concat_axis=0, tiled=True)]
    all_to_all x1, waiting for transfers between devices: 16.3 us -> 11.1 us  [spread(): return lax.all_to_all(copies, axes, split_axis=0, concat_axis=0, tiled=True)]
    dot_general x6 -> x0, matrix products: 3.57 us -> none  [the longest x1 0.63 us: local(): jnp.dot(panel_in, up_masked, preferred_element_type=jnp.float32)]
  transfers between devices with their start and end apart: 4 -> 3, of which waited for: 4 -> 3; matrix products, arithmetic and copies ran while one was open for 8% -> 1% of each run, Pallas kernels for 0% -> 3%
where the time goes in v2:
time: 143 us; the launch traced here: 142 us
  blocking collectives  75.7 us (53%)
  starting transfers between devices  25.1 us (18%)
  waiting for transfers between devices  21 us (15%)
  Pallas kernels  13.1 us (9%)
  local copies, waits for them, and re-layouts  4.09 us (3%)
  other arithmetic  2.19 us (2%)
    all_to_all x2, blocking collectives, swap(): return lax.all_to_all(blocks, axes, split_axis=0, concat_axis=0, tiled=True)  39.1 us
    all_to_all x2, blocking collectives, spread(): return lax.all_to_all(copies, axes, split_axis=0, concat_axis=0, tiled=True)  31.9 us
    all_to_all x1, starting transfers between devices, spread(): return lax.all_to_all(copies, axes, split_axis=0, concat_axis=0, tiled=True)  16.1 us
    all_to_all x1, waiting for transfers between devices, spread(): return lax.all_to_all(copies, axes, split_axis=0, concat_axis=0, tiled=True)  11.1 us
    all_to_all x1, waiting for transfers between devices, swap(): return lax.all_to_all(blocks, axes, split_axis=0, concat_axis=0, tiled=True)  8.4 us
    ppermute x1, starting transfers between devices, local(): got = lax.ppermute(give, 'core', [(0, 1), (1, 0)])  5.1 us
    all_gather x1, blocking collectives, local(): lax.all_gather(acts, 'core', axis=0, tiled=True)  4.78 us
    pallas_call x1, Pallas kernels, local(): pl.pallas_call(first_kernel, grid=(STEPS,), in_specs=[smem, smem, near_sp...  4.61 us
  transfers between devices with their start and end apart: 3, of which 3 were waited for; matrix products, arithmetic and copies ran while one was open for 1% of the time, Pallas kernels for 3%

profile of v2, /device:TPU:1, one launch (start us, length us, event | category | flops | bytes accessed | tf_op | source)
XLA Modules:
  0.0 142.0 jit_solution(6786588159566630028)
XLA Ops:
  0.6 0.7 pad_maximum_fusion.1
  1.4 0.7 broadcast_in_dim.8
  2.1 16.1 %all-to-all-start = ((bf16[8,2,4,1536]{3,2,1,0:T(4,128)(2,1)}), bf16[8,2,4,1536]{3,2,1,0:T(4,128)(2,1)S(1)}, u32[]{:S(2)}, u32[]{:S(2)}) async-start(bf16[8,2,4,1536]{3,2,1,0:T(4,128)(2,1)} %broadcast_in_dim.8), calls=%async_computation | async-start | bytes 393216 | tf_op jit(solution)/shard_map/all_to_all | solution.py:32
  18.2 1.4 dynamic_slice.3.mask_ref
  19.6 11.1 %all-to-all-done = bf16[8,2,4,1536]{3,2,1,0:T(4,128)(2,1)S(1)} async-done(((bf16[8,2,4,1536]{3,2,1,0:T(4,128)(2,1)}), bf16[8,2,4,1536]{3,2,1,0:T(4,128)(2,1)S(1)}, u32[]{:S(2)}, u32[]{:S(2)}) %all-to-all-start) | async-done | bytes 196640 | tf_op jit(solution)/shard_map/all_to_all | solution.py:32
  30.7 0.2 copy.14
  30.9 0.1 broadcast_in_dim.10
  31.1 23.7 %all_to_all.30.near_ref = bf16[8,2,32,1536]{3,2,1,0:T(8,128)(2,1)} all-to-all(bf16[8,2,32,1536]{3,2,1,0:T(8,128)(2,1)S(1)} %broadcast_in_dim.10), channel_id=1, replica_groups=mesh['zh'=4,'zl'=2,'x'=4,'yh'=2,'yl'=4,'core'=2] {'x','zl'}, dimensions={0} | all-to-all | bytes 3145728 | tf_op jit(solution)/shard_map/all_to_all | solution.py:32
  54.8 4.6 %partial_sums.1 = (f32[2,128,384]{2,1,0:T(8,128)}, f32[2,128,384]{2,1,0:T(8,128)}) custom-call(s32[1]{0:T(128)} %bitcast.2.core_ref, s32[12,3]{1,0:T(8,128)} %dynamic_slice.3.mask_ref, bf16[8,2,32,1536]{3,2,1,0:T(8,128)(2,1)} %all_to_all.30.near_ref, bf16[1536,384]{1,0:T(8,128)(2,1)} %up_ref.3, bf16[384,1536]{1,0:T(8,128)(2,1)} %down_ref.3), custom_call_target="tpu_custom_call" | custom-call | flops 603979776 | bytes 3932160 | tf_op jit(solution)/shard_map/partial_sums/pallas_call | solution.py:151
  59.4 5.1 %collective-permute-start = (f32[2,128,384]{2,1,0:T(8,128)}, f32[2,128,384]{2,1,0:T(8,128)S(1)}, u32[]{:S(2)}, u32[]{:S(2)}) collective-permute-start(f32[2,128,384]{2,1,0:T(8,128)} %get-tuple-element.19), channel_id=1, source_target_pairs={{0,1},{1,0},{2,3},{3,2},{4,5},{5,4},{6,7},{7,6},{8,9},{9,8},{10,11... | collective-permute-start | bytes 1179656 | tf_op jit(solution)/shard_map/ppermute | solution.py:166
  64.5 1.5 %collective-permute-done = f32[2,128,384]{2,1,0:T(8,128)S(1)} collective-permute-done((f32[2,128,384]{2,1,0:T(8,128)}, f32[2,128,384]{2,1,0:T(8,128)S(1)}, u32[]{:S(2)}, u32[]{:S(2)}) %collective-permute-start) | collective-permute-done | bytes 393248 | tf_op jit(solution)/shard_map/ppermute | solution.py:166
  66.0 1.0 add.46
  67.1 14.5 %all_to_all.31 = f32[4,2,32,384]{3,2,1,0:T(8,128)S(1)} all-to-all(f32[4,2,32,384]{3,2,1,0:T(8,128)S(1)} %bitcast.20), channel_id=1, replica_groups=mesh['zh'=4,'zl'=2,'x'=4,'yh'=2,'yl'=4,'core'=2] {'yl'}, dimensions={0} | all-to-all | bytes 786432 | tf_op jit(solution)/shard_map/all_to_all | solution.py:36
  81.7 8.2 %all_to_all.32 = bf16[4,2,32,384]{3,2,1,0:T(8,128)(2,1)S(1)} all-to-all(bf16[4,2,32,384]{3,2,1,0:T(8,128)(2,1)S(1)} %broadcast_in_dim.22), channel_id=1, replica_groups=mesh['zh'=4,'zl'=2,'x'=4,'yh'=2,'yl'=4,'core'=2] {'yl'}, dimensions={0} | all-to-all | bytes 393216 | tf_op jit(solution)/shard_map/all_to_all | solution.py:32
  89.9 4.8 %all_gather.3 = bf16[2,256,384]{2,1,0:T(8,128)(2,1)} all-gather(bf16[1,256,384]{2,1,0:T(8,128)(2,1)S(1)} %bitcast.25), channel_id=1, replica_groups=mesh['zh'=4,'zl'=2,'x'=4,'yh'=2,'yl'=4,'core'=2] {'core'}, dimensions={0}, use_global_device_ids=true | all-gather | bytes 589824 | tf_op jit(solution)/shard_map/all_gather | solution.py:173
  94.7 4.4 %output_terms.1 = bf16[8,2,32,1536]{3,2,1,0:T(8,128)(2,1)} custom-call(s32[12,3]{1,0:T(8,128)} %dynamic_slice.3.mask_ref, bf16[8,2,32,384]{3,2,1,0:T(8,128)(2,1)} %bitcast.18, bf16[1536,384]{1,0:T(8,128)(2,1)} %up_ref.3, bf16[384,1536]{1,0:T(8,128)(2,1)} %down_ref.3), custom_call_target="tpu_custom_call" | custom-call | flops 603979776 | bytes 3932160 | tf_op jit(solution)/shard_map/output_terms/pallas_call | solution.py:175
  99.2 24.6 %all_to_all.33 = bf16[8,2,32,1536]{3,2,1,0:T(8,128)(2,1)S(1)} all-to-all(bf16[8,2,32,1536]{3,2,1,0:T(8,128)(2,1)} %output_terms.1), channel_id=1, replica_groups=mesh['zh'=4,'zl'=2,'x'=4,'yh'=2,'yl'=4,'core'=2] {'x','zl'}, dimensions={0} | all-to-all | bytes 3145728 | tf_op jit(solution)/shard_map/all_to_all | solution.py:36
  123.7 0.2 reduce_sum.34
  124.0 0.2 copy.17
  124.2 0.8 copy.18
  124.9 3.9 %all-to-all-start.5 = ((bf16[8,2,4,1536]{3,2,1,0:T(4,128)(2,1)}), bf16[8,2,4,1536]{3,2,1,0:T(4,128)(2,1)S(1)}, u32[]{:S(2)}, u32[]{:S(2)}) async-start(bf16[8,2,4,1536]{3,2,1,0:T(4,128)(2,1)} %copy.18), calls=%async_computation.5 | async-start | bytes 393216 | tf_op jit(solution)/shard_map/all_to_all | solution.py:36
  128.8 4.0 %weight_grads.1 = (bf16[1536,384]{1,0:T(8,128)(2,1)}, bf16[384,1536]{1,0:T(8,128)(2,1)}) custom-call(s32[12,3]{1,0:T(8,128)} %dynamic_slice.3.mask_ref, bf16[8,2,32,384]{3,2,1,0:T(8,128)(2,1)} %bitcast.19, bf16[8,2,32,1536]{3,2,1,0:T(8,128)(2,1)} %all_to_all.30.near_ref), custom_call_target="tpu_custom_call" | custom-call | flops 603979776 | bytes 3932160 | tf_op jit(solution)/shard_map/weight_grads/pallas_call | solution.py:193
  132.9 8.4 %all-to-all-done.5 = bf16[8,2,4,1536]{3,2,1,0:T(4,128)(2,1)S(1)} async-done(((bf16[8,2,4,1536]{3,2,1,0:T(4,128)(2,1)}), bf16[8,2,4,1536]{3,2,1,0:T(4,128)(2,1)S(1)}, u32[]{:S(2)}, u32[]{:S(2)}) %all-to-all-start.5) | async-done | bytes 196640 | tf_op jit(solution)/shard_map/all_to_all | solution.py:36
  141.4 0.6 slice_bitcast_fusion
  (7 shorter events, 0.2 us)
Async XLA Ops:
  2.1 28.6 %all-to-all-start = ((bf16[8,2,4,1536]{3,2,1,0:T(4,128)(2,1)}), bf16[8,2,4,1536]{3,2,1,0:T(4,128)(2,1)S(1)}, u32[]{:S(2)}, u32[]{:S(2)}) async-start(bf16[8,2,4,1536]{3,2,1,0:T(4,128)(2,1)} %broadcast_in_dim.8), calls=%async_computation | async-start | bytes 393216 | tf_op jit(solution)/shard_map/all_to_all | solution.py:32
  59.4 6.7 %collective-permute-start = (f32[2,128,384]{2,1,0:T(8,128)}, f32[2,128,384]{2,1,0:T(8,128)S(1)}, u32[]{:S(2)}, u32[]{:S(2)}) collective-permute-start(f32[2,128,384]{2,1,0:T(8,128)} %get-tuple-element.19), channel_id=1, source_target_pairs={{0,1},{1,0},{2,3},{3,2},{4,5},{5,4},{6,7},{7,6},{8,9},{9,8},{10,11... | collective-permute-start | bytes 1179656 | tf_op jit(solution)/shard_map/ppermute | solution.py:166
  124.9 16.3 %all-to-all-start.5 = ((bf16[8,2,4,1536]{3,2,1,0:T(4,128)(2,1)}), bf16[8,2,4,1536]{3,2,1,0:T(4,128)(2,1)S(1)}, u32[]{:S(2)}, u32[]{:S(2)}) async-start(bf16[8,2,4,1536]{3,2,1,0:T(4,128)(2,1)} %copy.18), calls=%async_computation.5 | async-start | bytes 393216 | tf_op jit(solution)/shard_map/all_to_all | solution.py:36

commit v3 on v1

v3 whole, which is shorter than its diff:
```python
import jax
import jax.numpy as jnp
from jax import lax
from jax.experimental import pallas as pl
from jax.experimental.pallas import tpu as pltpu
from jax.sharding import Mesh, PartitionSpec as P

BLK = 128
AXES = ("zh", "zl", "xh", "xl", "yh", "ylh", "yll", "core")
SIZES = (4, 2, 2, 2, 2, 2, 2, 2)
ROW = ("zh", "zl", "xh", "xl", "yh")
COL = ("ylh", "yll", "core")
FAR = ("yh", "zh")
NEAR = ("xl", "xh", "zl")
LINE = ("yll", "ylh")
VMEM_BYTES = 16 * 1024 * 1024

slope_coef = 0.7978845608
cubic_coef = 0.044715


def gelu_pair(values):
    tangent = jnp.tanh(slope_coef * (values + cubic_coef * values * values * values))
    value = 0.5 * values * (1.0 + tangent)
    slope = 0.5 * (1.0 + tangent) + 0.5 * values * (1.0 - tangent * tangent) * slope_coef * (
        1.0 + 3.0 * cubic_coef * values * values
    )
    return value, slope


def spread(block, axes, count):
    copies = jnp.broadcast_to(block[None], (count,) + block.shape)
    return lax.all_to_all(copies, axes, split_axis=0, concat_axis=0, tiled=True)


def swap(blocks, axes):
    return lax.all_to_all(blocks, axes, split_axis=0, concat_axis=0, tiled=True)


def kept(mask_ref, d_block, f_block, block):
    return jnp.where(mask_ref[d_block, f_block] != 0, block, jnp.zeros_like(block))


def dot(a, b, axis_a, axis_b):
    dims = (((axis_a,), (axis_b,)), ((), ()))
    return lax.dot_general(a, b, dims, preferred_element_type=jnp.float32)


def first_kernel(core_ref, mask_ref, near_ref, up_ref, down_ref, keep_ref, give_ref, um, dm):
    width, units = um.shape
    for i in range(width // BLK):
        d = slice(i * BLK, (i + 1) * BLK)
        for j in range(units // BLK):
            f = slice(j * BLK, (j + 1) * BLK)
            um[d, f] = kept(mask_ref, i, j, up_ref[d, f])
            dm[f, d] = kept(mask_ref, i, j, down_ref[f, d])
    half = keep_ref.shape[1]
    hidden = dot(near_ref[:, 0].reshape(2 * half, width), um[...], 1, 0)
    grad = dot(near_ref[:, 1].reshape(2 * half, width), dm[...], 1, 1)
    low = core_ref[0] == 0
    for k, part in enumerate((hidden, grad)):
        a, b = part[:half], part[half:]
        keep_ref[k] = jnp.where(low, a, b)
        give_ref[k] = jnp.where(low, b, a)


def second_kernel(acts_ref, um, dm, terms_ref):
    blocks, _, rows, units = acts_ref.shape
    width = um.shape[0]
    wide = width // 3
    act = acts_ref[:, 0].reshape(blocks * rows, units)
    dact = acts_ref[:, 1].reshape(blocks * rows, units)
    for k in range(3):
        w = slice(k * wide, (k + 1) * wide)
        out = dot(act, dm[:, w], 1, 0).astype(terms_ref.dtype)
        terms_ref[:, 0, :, w] = out.reshape(blocks, rows, wide)
        back = dot(dact, um[w, :], 1, 1).astype(terms_ref.dtype)
        terms_ref[:, 1, :, w] = back.reshape(blocks, rows, wide)


def third_kernel(mask_ref, acts_ref, near_ref, upg_ref, downg_ref):
    blocks, _, rows, units = acts_ref.shape
    width = upg_ref.shape[0]
    wide = width // 3
    tokens = blocks * rows
    act = acts_ref[:, 0].reshape(tokens, units)
    dact = acts_ref[:, 1].reshape(tokens, units)
    for k in range(3):
        w = slice(k * wide, (k + 1) * wide)
        down = dot(act, near_ref[:, 1, :, w].reshape(tokens, wide), 0, 0).astype(downg_ref.dtype)
        up = dot(near_ref[:, 0, :, w].reshape(tokens, wide), dact, 0, 0).astype(upg_ref.dtype)
        for i in range(wide // BLK):
            d = slice(i * BLK, (i + 1) * BLK)
            at = slice(k * wide + i * BLK, k * wide + (i + 1) * BLK)
            for j in range(units // BLK):
                f = slice(j * BLK, (j + 1) * BLK)
                d_block = k * (wide // BLK) + i
                upg_ref[at, f] = kept(mask_ref, d_block, j, up[d, f])
                downg_ref[f, at] = kept(mask_ref, d_block, j, down[f, d])


def local(inputs, up_weight, down_weight, out_grad, block_mask):
    row_index = lax.axis_index(ROW)
    col_index = lax.axis_index(COL)
    core = lax.axis_index("core")
    rows, width = inputs.shape
    units = up_weight.shape[1]
    d_blocks = width // BLK
    f_blocks = units // BLK
    tokens = 64 * rows
    half = tokens // 2
    quarter = half // 4
    bf, f4 = jnp.bfloat16, jnp.float32
    smem = pl.BlockSpec(memory_space=pltpu.SMEM)
    vmem = pl.BlockSpec(memory_space=pltpu.VMEM)
    params = pltpu.CompilerParams(vmem_limit_bytes=VMEM_BYTES)
    cost = pl.CostEstimate(
        flops=4 * tokens * width * units,
        bytes_accessed=4 * width * (units + tokens),
        transcendentals=0,
    )
    masked = [jax.ShapeDtypeStruct((width, units), bf), jax.ShapeDtypeStruct((units, width), bf)]

    both = jnp.stack([inputs, out_grad])
    far = spread(both, FAR, 8)
    mask = lax.dynamic_slice(
        block_mask, (col_index * d_blocks, row_index * f_blocks), (d_blocks, f_blocks)
    )
    far, mask = lax.optimization_barrier((far, mask))
    far = far.transpose(1, 0, 2, 3).reshape(2, 8 * rows, width)
    near = spread(far, NEAR, 8)

    keep, give, up_masked, down_masked = pl.pallas_call(
        first_kernel,
        in_specs=[smem, smem, vmem, vmem, vmem],
        out_specs=[vmem] * 4,
        out_shape=[jax.ShapeDtypeStruct((2, half, units), f4)] * 2 + masked,
        compiler_params=params,
        cost_estimate=cost,
        name="partial_sums",
    )(core.reshape(1), mask, near, up_weight, down_weight)
    pair = keep + lax.ppermute(give, "core", [(0, 1), (1, 0)])
    pair = pair.reshape(2, 4, quarter, units).transpose(1, 0, 2, 3)
    sent = pair.astype(bf)
    lost = lax.dynamic_index_in_dim(pair, lax.axis_index(LINE), 0, keepdims=False)
    lost = lost - lost.astype(bf).astype(f4)
    sent, lost = lax.optimization_barrier((sent, lost))
    summed = jnp.sum(swap(sent, LINE).astype(f4), axis=0) + lost
    value, slope = gelu_pair(summed[0])
    acts = jnp.stack([value, summed[1] * slope]).astype(bf)
    acts = spread(acts, LINE, 4).reshape(1, 8 * quarter, units)
    acts = lax.all_gather(acts, "core", axis=0, tiled=True).reshape(8, 2, quarter, units)

    terms = pl.pallas_call(
        second_kernel,
        in_specs=[vmem] * 3,
        out_specs=vmem,
        out_shape=jax.ShapeDtypeStruct((8, 2, 8 * rows, width), bf),
        compiler_params=params,
        cost_estimate=cost,
        name="output_terms",
    )(acts, up_masked, down_masked)

    terms = swap(terms, NEAR)
    terms, acts, near = lax.optimization_barrier((terms, acts, near))
    sums = jnp.sum(terms.astype(f4), axis=0).astype(bf)
    sums = sums.reshape(2, 8, rows, width).transpose(1, 0, 2, 3)
    sums, acts, near = lax.optimization_barrier((sums, acts, near))
    sums = swap(sums, FAR)
    up_grad, down_grad = pl.pallas_call(
        third_kernel,
        in_specs=[smem, vmem, vmem],
        out_specs=[vmem, vmem],
        out_shape=masked,
        compiler_params=params,
        cost_estimate=cost,
        name="weight_grads",
    )(mask, acts, near)
    sums, up_grad, down_grad = lax.optimization_barrier((sums, up_grad, down_grad))
    totals = jnp.sum(sums.astype(f4), axis=0).astype(bf)
    return (totals[0], totals[1], up_grad, down_grad)


def solution(mesh):
    fine = Mesh(mesh.devices.reshape(SIZES), AXES)
    in_specs = (P(ROW, COL), P(COL, ROW), P(ROW, COL), P(ROW, COL), P())
    out_specs = (P(ROW, COL), P(ROW, COL), P(COL, ROW), P(ROW, COL))
    return jax.shard_map(local, mesh=fine, in_specs=in_specs, out_specs=out_specs, check_vma=False)
```

time: 136 us -> 134 us (0.985)
  the two profiles are of different devices: /device:TPU:1 before, /device:TPU:8 now
where the time goes in v3:
time: 134 us; the launch traced here: 133 us
  blocking collectives  71.9 us (54%)
  waiting for transfers between devices  26.3 us (20%)
  starting transfers between devices  20.7 us (15%)
  Pallas kernels  5.56 us (4%)
  local copies, waits for them, and re-layouts  4.5 us (3%)
  other arithmetic  3.64 us (3%)
    all_to_all x2, blocking collectives, spread(): return lax.all_to_all(copies, axes, split_axis=0, concat_axis=0, tiled=True)  35.2 us
    all_to_all x2, blocking collectives, swap(): return lax.all_to_all(blocks, axes, split_axis=0, concat_axis=0, tiled=True)  34.7 us
    all_to_all x1, starting transfers between devices, spread(): return lax.all_to_all(copies, axes, split_axis=0, concat_axis=0, tiled=True)  14.7 us
    all_to_all x1, waiting for transfers between devices, spread(): return lax.all_to_all(copies, axes, split_axis=0, concat_axis=0, tiled=True)  14.1 us
    all_to_all x1, waiting for transfers between devices, swap(): return lax.all_to_all(blocks, axes, split_axis=0, concat_axis=0, tiled=True)  10.3 us
    all_to_all x1, starting transfers between devices, swap(): return lax.all_to_all(blocks, axes, split_axis=0, concat_axis=0, tiled=True)  4.14 us
    pallas_call x1, Pallas kernels, local(): pl.pallas_call(third_kernel, in_specs=[smem, vmem, vmem], out_specs=[vmem...  2.85 us
  transfers between devices with their start and end apart: 3, of which 3 were waited for; matrix products, arithmetic and copies ran while one was open for 1% of the time, Pallas kernels for 2%

profile of v3, /device:TPU:8, one launch (start us, length us, event | category | flops | bytes accessed | tf_op | source)
XLA Modules:
  0.0 133.4 jit_solution(5511944886743828475)
XLA Ops:
  0.6 0.7 pad_maximum_fusion.1
  1.4 0.7 broadcast_in_dim.8
  2.1 14.7 %all-to-all-start = ((bf16[8,2,4,1536]{3,2,1,0:T(4,128)(2,1)}), bf16[8,2,4,1536]{3,2,1,0:T(4,128)(2,1)S(1)}, u32[]{:S(2)}, u32[]{:S(2)}) async-start(bf16[8,2,4,1536]{3,2,1,0:T(4,128)(2,1)} %broadcast_in_dim.8), calls=%async_computation | async-start | bytes 393216 | tf_op jit(solution)/shard_map/all_to_all | solution.py:33
  16.8 0.8 dynamic_slice.5.mask_ref
  17.6 14.1 %all-to-all-done = bf16[8,2,4,1536]{3,2,1,0:T(4,128)(2,1)S(1)} async-done(((bf16[8,2,4,1536]{3,2,1,0:T(4,128)(2,1)}), bf16[8,2,4,1536]{3,2,1,0:T(4,128)(2,1)S(1)}, u32[]{:S(2)}, u32[]{:S(2)}) %all-to-all-start) | async-done | bytes 196640 | tf_op jit(solution)/shard_map/all_to_all | solution.py:33
  31.7 0.2 copy.14
  32.1 25.6 %all_to_all.30.near_ref = bf16[8,2,32,1536]{3,2,1,0:T(8,128)(2,1)S(1)} all-to-all(bf16[8,2,32,1536]{3,2,1,0:T(8,128)(2,1)S(1)} %broadcast_in_dim.10), channel_id=1, replica_groups=mesh['zh'=4,'zl'=2,'xh'=2,'xl'=2,'yh'=2,'ylh'=2,'yll'=2,'core'=2] {'xl',..., dimensions={0} | all-to-all | bytes 3145728 | tf_op jit(solution)/shard_map/all_to_all | solution.py:33
  57.7 1.7 %partial_sums.1 = (f32[2,128,384]{2,1,0:T(8,128)S(1)}, f32[2,128,384]{2,1,0:T(8,128)S(1)}, bf16[1536,384]{1,0:T(8,128)(2,1)S(1)}, bf16[384,1536]{1,0:T(8,128)(2,1)S(1)}) custom-call(s32[1]{0:T(128)} %bitcast.core_ref, s32[12,3]{1,0:T(8,128)S(1)} %dynamic_slice.5.mask_ref, bf16[8,2,32,1536]{3,2,1,0:T(8,128)(2,1)S(1)} %all_to_all.30.near_ref, ...), custom_call_target="tpu_custom_call" | custom-call | flops 603979776 | bytes 3932160 | tf_op jit(solution)/shard_map/partial_sums/pallas_call | solution.py:133
  59.5 1.0 copy-done.2
  60.5 1.9 %collective-permute-start = (f32[2,128,384]{2,1,0:T(8,128)S(1)}, f32[2,128,384]{2,1,0:T(8,128)}, u32[]{:S(2)}, u32[]{:S(2)}) collective-permute-start(f32[2,128,384]{2,1,0:T(8,128)S(1)} %get-tuple-element.26), channel_id=1, source_target_pairs={{0,1},{1,0},{2,3},{3,2},{4,5},{5,4},{6,7},{7,6},{8,9},{9,8},{10,11... | collective-permute-start | bytes 1179656 | tf_op jit(solution)/shard_map/ppermute | solution.py:142
  62.4 1.8 %collective-permute-done = f32[2,128,384]{2,1,0:T(8,128)} collective-permute-done((f32[2,128,384]{2,1,0:T(8,128)S(1)}, f32[2,128,384]{2,1,0:T(8,128)}, u32[]{:S(2)}, u32[]{:S(2)}) %collective-permute-start) | collective-permute-done | bytes 393248 | tf_op jit(solution)/shard_map/ppermute | solution.py:142
  64.2 1.0 add.64
  65.3 9.4 %all_to_all.31 = bf16[4,2,32,384]{3,2,1,0:T(8,128)(2,1)S(1)} all-to-all(bf16[4,2,32,384]{3,2,1,0:T(8,128)(2,1)S(1)} %bitcast.30), channel_id=1, replica_groups=mesh['zh'=4,'zl'=2,'xh'=2,'xl'=2,'yh'=2,'ylh'=2,'yll'=2,'core'=2] {'yll'..., dimensions={0} | all-to-all | bytes 393216 | tf_op jit(solution)/shard_map/all_to_all | solution.py:37
  74.8 9.5 %all_to_all.32 = bf16[4,2,32,384]{3,2,1,0:T(8,128)(2,1)S(1)} all-to-all(bf16[4,2,32,384]{3,2,1,0:T(8,128)(2,1)S(1)} %broadcast_in_dim.22), channel_id=1, replica_groups=mesh['zh'=4,'zl'=2,'xh'=2,'xl'=2,'yh'=2,'ylh'=2,'yll'=2,'core'=2] {'yll'..., dimensions={0} | all-to-all | bytes 393216 | tf_op jit(solution)/shard_map/all_to_all | solution.py:33
  84.4 2.1 %all_gather.3 = bf16[2,256,384]{2,1,0:T(8,128)(2,1)S(1)} all-gather(bf16[1,256,384]{2,1,0:T(8,128)(2,1)S(1)} %bitcast.31), channel_id=1, replica_groups=mesh['zh'=4,'zl'=2,'xh'=2,'xl'=2,'yh'=2,'ylh'=2,'yll'=2,'core'=2] {'core'}, dimensions={0}, use_global_device_ids=true | all-gather | bytes 589824 | tf_op jit(solution)/shard_map/all_gather | solution.py:152
  86.4 1.0 output_terms.1
  87.4 25.3 %all_to_all.33 = bf16[8,2,32,1536]{3,2,1,0:T(8,128)(2,1)} all-to-all(bf16[8,2,32,1536]{3,2,1,0:T(8,128)(2,1)S(1)} %output_terms.1), channel_id=1, replica_groups=mesh['zh'=4,'zl'=2,'xh'=2,'xl'=2,'yh'=2,'ylh'=2,'yll'=2,'core'=2] {'xl',..., dimensions={0} | all-to-all | bytes 3145728 | tf_op jit(solution)/shard_map/all_to_all | solution.py:37
  112.7 1.6 %reduce_sum.34 = bf16[2,32,1536]{2,1,0:T(8,128)(2,1)S(1)} reduce(bf16[8,2,32,1536]{3,2,1,0:T(8,128)(2,1)} %all_to_all.33, bf16[]{:T(256)} %constant.66.clone.1), dimensions={0}, to_apply=%region_1.2 | reduce | flops 688128 | bytes 1769474 | tf_op jit(solution)/shard_map/reduce_sum | solution.py:166
  114.4 0.2 copy.17
  114.6 0.8 copy.18
  115.3 4.1 %all-to-all-start.5 = ((bf16[8,2,4,1536]{3,2,1,0:T(4,128)(2,1)}), bf16[8,2,4,1536]{3,2,1,0:T(4,128)(2,1)S(1)}, u32[]{:S(2)}, u32[]{:S(2)}) async-start(bf16[8,2,4,1536]{3,2,1,0:T(4,128)(2,1)} %copy.18), calls=%async_computation.5 | async-start | bytes 393216 | tf_op jit(solution)/shard_map/all_to_all | solution.py:37
  119.5 2.8 %weight_grads.1 = (bf16[1536,384]{1,0:T(8,128)(2,1)}, bf16[384,1536]{1,0:T(8,128)(2,1)}) custom-call(s32[12,3]{1,0:T(8,128)S(1)} %dynamic_slice.5.mask_ref, bf16[8,2,32,384]{3,2,1,0:T(8,128)(2,1)S(1)} %bitcast.24, bf16[8,2,32,1536]{3,2,1,0:T(8,128)(2,1)S(1)} %all_to_all.30.near_ref), custom_call_target="tpu_custom_call" | custom-call | flops 603979776 | bytes 3932160 | tf_op jit(solution)/shard_map/weight_grads/pallas_call | solution.py:170
  122.3 10.3 %all-to-all-done.5 = bf16[8,2,4,1536]{3,2,1,0:T(4,128)(2,1)S(1)} async-done(((bf16[8,2,4,1536]{3,2,1,0:T(4,128)(2,1)}), bf16[8,2,4,1536]{3,2,1,0:T(4,128)(2,1)S(1)}, u32[]{:S(2)}, u32[]{:S(2)}) %all-to-all-start.5) | async-done | bytes 196640 | tf_op jit(solution)/shard_map/all_to_all | solution.py:37
  132.8 0.6 slice_bitcast_fusion
  (17 shorter events, 0.4 us)
Async XLA Ops:
  2.1 29.6 %all-to-all-start = ((bf16[8,2,4,1536]{3,2,1,0:T(4,128)(2,1)}), bf16[8,2,4,1536]{3,2,1,0:T(4,128)(2,1)S(1)}, u32[]{:S(2)}, u32[]{:S(2)}) async-start(bf16[8,2,4,1536]{3,2,1,0:T(4,128)(2,1)} %broadcast_in_dim.8), calls=%async_computation | async-start | bytes 393216 | tf_op jit(solution)/shard_map/all_to_all | solution.py:33
  32.0 25.7 %copy-start = (bf16[1536,384]{1,0:T(8,128)(2,1)S(1)}, bf16[1536,384]{1,0:T(8,128)(2,1)}, u32[]{:S(2)}) copy-start(bf16[1536,384]{1,0:T(8,128)(2,1)} %up_ref.1) | copy-start | bytes 3538948
  32.0 25.7 %copy-start.1 = (bf16[384,1536]{1,0:T(8,128)(2,1)S(1)}, bf16[384,1536]{1,0:T(8,128)(2,1)}, u32[]{:S(2)}) copy-start(bf16[384,1536]{1,0:T(8,128)(2,1)} %down_ref.1) | copy-start | bytes 3538948
  59.5 1.0 copy-start.2
  60.5 3.7 %collective-permute-start = (f32[2,128,384]{2,1,0:T(8,128)S(1)}, f32[2,128,384]{2,1,0:T(8,128)}, u32[]{:S(2)}, u32[]{:S(2)}) collective-permute-start(f32[2,128,384]{2,1,0:T(8,128)S(1)} %get-tuple-element.26), channel_id=1, source_target_pairs={{0,1},{1,0},{2,3},{3,2},{4,5},{5,4},{6,7},{7,6},{8,9},{9,8},{10,11... | collective-permute-start | bytes 1179656 | tf_op jit(solution)/shard_map/ppermute | solution.py:142
  65.3 21.1 %copy-start.3 = (bf16[384,1536]{1,0:T(8,128)(2,1)S(1)}, bf16[384,1536]{1,0:T(8,128)(2,1)}, u32[]{:S(2)}) copy-start(bf16[384,1536]{1,0:T(8,128)(2,1)} %copy-done.2) | copy-start | bytes 3538948
  115.3 17.3 %all-to-all-start.5 = ((bf16[8,2,4,1536]{3,2,1,0:T(4,128)(2,1)}), bf16[8,2,4,1536]{3,2,1,0:T(4,128)(2,1)S(1)}, u32[]{:S(2)}, u32[]{:S(2)}) async-start(bf16[8,2,4,1536]{3,2,1,0:T(4,128)(2,1)} %copy.18), calls=%async_computation.5 | async-start | bytes 393216 | tf_op jit(solution)/shard_map/all_to_all | solution.py:37

commit v4 on v3

--- a/solution.py
+++ b/solution.py
@@ -1,5 +1,8 @@
+import math
+
 import jax
 import jax.numpy as jnp
+import numpy as np
 from jax import lax
 from jax.experimental import pallas as pl
 from jax.experimental.pallas import tpu as pltpu
@@ -10,10 +13,11 @@
 SIZES = (4, 2, 2, 2, 2, 2, 2, 2)
 ROW = ("zh", "zl", "xh", "xl", "yh")
 COL = ("ylh", "yll", "core")
-FAR = ("yh", "zh")
-NEAR = ("xl", "xh", "zl")
+FAR = ("xh", "zh", "yh")
+FARS = 16
+NEARS = 4
 LINE = ("yll", "ylh")
-VMEM_BYTES = 16 * 1024 * 1024
+VMEM_BYTES = 10 * 1024 * 1024
 
 slope_coef = 0.7978845608
 cubic_coef = 0.044715
@@ -28,6 +32,22 @@
     return value, slope
 
 
+def near_groups():
+    order = np.arange(math.prod(SIZES)).reshape(8, 4, 2, 4, 2)
+    groups = []
+    for yh, yl, core, zp, xp in np.ndindex(2, 4, 2, 4, 2):
+        zs = sorted(((2 * zp + core) % 8, (2 * zp + core + 1) % 8), key=lambda z: z % 2)
+        xs = sorted(((2 * xp + core) % 4, (2 * xp + core + 1) % 4), key=lambda x: x % 2)
+        groups.append([int(order[z, x, yh, yl, core]) for x in xs for z in zs])
+    return groups
+
+
+def near_swap(blocks):
+    return lax.all_to_all(
+        blocks, AXES, split_axis=0, concat_axis=0, tiled=True, axis_index_groups=near_groups()
+    )
+
+
 def spread(block, axes, count):
     copies = jnp.broadcast_to(block[None], (count,) + block.shape)
     return lax.all_to_all(copies, axes, split_axis=0, concat_axis=0, tiled=True)
@@ -46,7 +66,7 @@
     return lax.dot_general(a, b, dims, preferred_element_type=jnp.float32)
 
 
-def first_kernel(core_ref, mask_ref, near_ref, up_ref, down_ref, keep_ref, give_ref, um, dm):
+def mask_weights(mask_ref, up_ref, down_ref, um, dm):
     width, units = um.shape
     for i in range(width // BLK):
         d = slice(i * BLK, (i + 1) * BLK)
@@ -54,6 +74,15 @@
             f = slice(j * BLK, (j + 1) * BLK)
             um[d, f] = kept(mask_ref, i, j, up_ref[d, f])
             dm[f, d] = kept(mask_ref, i, j, down_ref[f, d])
+
+
+def first_kernel(
+    core_ref, mask_ref, near_ref, up_ref, down_ref, keep_ref, give_ref, saved_ref, um, dm, sem
+):
+    saving = pltpu.make_async_copy(near_ref, saved_ref, sem)
+    saving.start()
+    mask_weights(mask_ref, up_ref, down_ref, um, dm)
+    width = um.shape[0]
     half = keep_ref.shape[1]
     hidden = dot(near_ref[:, 0].reshape(2 * half, width), um[...], 1, 0)
     grad = dot(near_ref[:, 1].reshape(2 * half, width), dm[...], 1, 1)
@@ -62,14 +91,17 @@
         a, b = part[:half], part[half:]
         keep_ref[k] = jnp.where(low, a, b)
         give_ref[k] = jnp.where(low, b, a)
-
-
-def second_kernel(acts_ref, um, dm, terms_ref):
+    saving.wait()
+
+
+def second_kernel(mask_ref, acts_ref, up_ref, down_ref, terms_ref, um, dm):
+    mask_weights(mask_ref, up_ref, down_ref, um, dm)
     blocks, _, rows, units = acts_ref.shape
     width = um.shape[0]
     wide = width // 3
     act = acts_ref[:, 0].reshape(blocks * rows, units)
     dact = acts_ref[:, 1].reshape(blocks * rows, units)
+    blocks, _, rows, _ = terms_ref.shape
     for k in range(3):
         w = slice(k * wide, (k + 1) * wide)
         out = dot(act, dm[:, w], 1, 0).astype(terms_ref.dtype)
@@ -119,22 +151,25 @@
         bytes_accessed=4 * width * (units + tokens),
         transcendentals=0,
     )
+    scratch = [pltpu.VMEM((width, units), bf), pltpu.VMEM((units, width), bf)]
     masked = [jax.ShapeDtypeStruct((width, units), bf), jax.ShapeDtypeStruct((units, width), bf)]
 
     both = jnp.stack([inputs, out_grad])
-    far = spread(both, FAR, 8)
+    far = spread(both, FAR, FARS)
     mask = lax.dynamic_slice(
         block_mask, (col_index * d_blocks, row_index * f_blocks), (d_blocks, f_blocks)
     )
     far, mask = lax.optimization_barrier((far, mask))
-    far = far.transpose(1, 0, 2, 3).reshape(2, 8 * rows, width)
-    near = spread(far, NEAR, 8)
-
-    keep, give, up_masked, down_masked = pl.pallas_call(
+    far = far.transpose(1, 0, 2, 3).reshape(1, 2, FARS * rows, width)
+    near = near_swap(jnp.broadcast_to(far, (NEARS,) + far.shape[1:]))
+
+    keep, give, saved = pl.pallas_call(
         first_kernel,
         in_specs=[smem, smem, vmem, vmem, vmem],
-        out_specs=[vmem] * 4,
-        out_shape=[jax.ShapeDtypeStruct((2, half, units), f4)] * 2 + masked,
+        out_specs=[vmem, vmem, pl.BlockSpec(memory_space=pltpu.HBM)],
+        out_shape=[jax.ShapeDtypeStruct((2, half, units), f4)] * 2
+        + [jax.ShapeDtypeStruct(near.shape, bf)],
+        scratch_shapes=scratch + [pltpu.SemaphoreType.DMA],
         compiler_params=params,
         cost_estimate=cost,
         name="partial_sums",
@@ -153,19 +188,20 @@
 
     terms = pl.pallas_call(
         second_kernel,
-        in_specs=[vmem] * 3,
+        in_specs=[smem, vmem, vmem, vmem],
         out_specs=vmem,
-        out_shape=jax.ShapeDtypeStruct((8, 2, 8 * rows, width), bf),
+        out_shape=jax.ShapeDtypeStruct((NEARS, 2, FARS * rows, width), bf),
+        scratch_shapes=scratch,
         compiler_params=params,
         cost_estimate=cost,
         name="output_terms",
-    )(acts, up_masked, down_masked)
-
-    terms = swap(terms, NEAR)
-    terms, acts, near = lax.optimization_barrier((terms, acts, near))
+    )(mask, acts, up_weight, down_weight)
+
+    terms = near_swap(terms)
+    terms, acts, saved = lax.optimization_barrier((terms, acts, saved))
     sums = jnp.sum(terms.astype(f4), axis=0).astype(bf)
-    sums = sums.reshape(2, 8, rows, width).transpose(1, 0, 2, 3)
-    sums, acts, near = lax.optimization_barrier((sums, acts, near))
+    sums = sums.reshape(2, FARS, rows, width).transpose(1, 0, 2, 3)
+    sums, acts, saved = lax.optimization_barrier((sums, acts, saved))
     sums = swap(sums, FAR)
     up_grad, down_grad = pl.pallas_call(
         third_kernel,
@@ -175,7 +211,7 @@
         compiler_params=params,
         cost_estimate=cost,
         name="weight_grads",
-    )(mask, acts, near)
+    )(mask, acts, saved)
     sums, up_grad, down_grad = lax.optimization_barrier((sums, up_grad, down_grad))
     totals = jnp.sum(sums.astype(f4), axis=0).astype(bf)
     return (totals[0], totals[1], up_grad, down_grad)

time: 134 us -> 130 us (0.970)
  blocking collectives: 71.9 us -> 51.6 us
  waiting for transfers between devices: 26.3 us -> 37.7 us
  starting transfers between devices: 20.7 us -> 26.7 us
  other arithmetic: 3.64 us -> 1.33 us
    all_to_all x0 -> x2, blocking collectives: none -> 30.5 us  [near_swap(): lax.all_to_all(blocks, AXES, split_axis=0, concat_axis=0, tiled=True, axi...]
    all_to_all x2 -> x1, blocking collectives: 35.2 us -> 9.52 us  [spread(): return lax.all_to_all(copies, axes, split_axis=0, concat_axis=0, tiled=True)]
    all_to_all x2 -> x1, blocking collectives: 34.7 us -> 9.46 us  [swap(): return lax.all_to_all(blocks, axes, split_axis=0, concat_axis=0, tiled=True)]
    all_to_all x1, waiting for transfers between devices: 10.3 us -> 17.7 us  [swap(): return lax.all_to_all(blocks, axes, split_axis=0, concat_axis=0, tiled=True)]
    all_to_all x1, waiting for transfers between devices: 14.1 us -> 18.7 us  [spread(): return lax.all_to_all(copies, axes, split_axis=0, concat_axis=0, tiled=True)]
    all_to_all x1, starting transfers between devices: 14.7 us -> 17.2 us  [spread(): return lax.all_to_all(copies, axes, split_axis=0, concat_axis=0, tiled=True)]
    all_to_all x1, starting transfers between devices: 4.14 us -> 6.5 us  [swap(): return lax.all_to_all(blocks, axes, split_axis=0, concat_axis=0, tiled=True)]
    reduce_sum x1, other arithmetic: 1.64 us -> 0.25 us  [local(): sums = jnp.sum(terms.astype(f4), axis=0).astype(bf)]
where the time goes in v4:
time: 130 us
  blocking collectives  51.6 us (40%)
  waiting for transfers between devices  37.7 us (29%)
  starting transfers between devices  26.7 us (21%)
  Pallas kernels  6.47 us (5%)
  local copies, waits for them, and re-layouts  5.28 us (4%)
  other arithmetic  1.33 us (1%)
    all_to_all x2, blocking collectives, near_swap(): lax.all_to_all(blocks, AXES, split_axis=0, concat_axis=0, tiled=True, axi...  30.5 us
    all_to_all x1, waiting for transfers between devices, spread(): return lax.all_to_all(copies, axes, split_axis=0, concat_axis=0, tiled=True)  18.7 us
    all_to_all x1, waiting for transfers between devices, swap(): return lax.all_to_all(blocks, axes, split_axis=0, concat_axis=0, tiled=True)  17.7 us
    all_to_all x1, starting transfers between devices, spread(): return lax.all_to_all(copies, axes, split_axis=0, concat_axis=0, tiled=True)  17.2 us
    all_to_all x1, blocking collectives, spread(): return lax.all_to_all(copies, axes, split_axis=0, concat_axis=0, tiled=True)  9.52 us
    all_to_all x1, blocking collectives, swap(): return lax.all_to_all(blocks, axes, split_axis=0, concat_axis=0, tiled=True)  9.46 us
    all_to_all x1, starting transfers between devices, swap(): return lax.all_to_all(blocks, axes, split_axis=0, concat_axis=0, tiled=True)  6.5 us
    ppermute x1, starting transfers between devices, local(): pair = keep + lax.ppermute(give, 'core', [(0, 1), (1, 0)])  2.92 us
  transfers between devices with their start and end apart: 3, of which 3 were waited for; matrix products, arithmetic and copies ran while one was open for 1% of the time, Pallas kernels for 2%

profile of v4, /device:TPU:8, one launch (start us, length us, event | category | flops | bytes accessed | tf_op | source)
XLA Modules:
  0.0 129.8 jit_solution(6572317832213129098)
XLA Ops:
  0.6 0.7 pad_maximum_fusion.1
  1.4 0.8 broadcast_in_dim.8
  2.2 17.2 %all-to-all-start = ((bf16[16,2,4,1536]{3,2,1,0:T(4,128)(2,1)}), bf16[16,2,4,1536]{3,2,1,0:T(4,128)(2,1)S(1)}, u32[]{:S(2)}, u32[]{:S(2)}) async-start(bf16[16,2,4,1536]{3,2,1,0:T(4,128)(2,1)} %broadcast_in_dim.8), calls=%async_computation | async-start | bytes 786432 | tf_op jit(solution)/shard_map/all_to_all | solution.py:53
  19.5 0.8 dynamic_slice.5.mask_ref
  20.3 18.7 %all-to-all-done = bf16[16,2,4,1536]{3,2,1,0:T(4,128)(2,1)S(1)} async-done(((bf16[16,2,4,1536]{3,2,1,0:T(4,128)(2,1)}), bf16[16,2,4,1536]{3,2,1,0:T(4,128)(2,1)S(1)}, u32[]{:S(2)}, u32[]{:S(2)}) %all-to-all-start) | async-done | bytes 393248 | tf_op jit(solution)/shard_map/all_to_all | solution.py:53
  39.0 0.3 copy.14
  39.5 15.3 %all_to_all.30.near_ref = bf16[4,2,64,1536]{3,2,1,0:T(8,128)(2,1)S(1)} all-to-all(bf16[4,2,64,1536]{3,2,1,0:T(8,128)(2,1)S(1)} %broadcast_in_dim.10), channel_id=1, replica_groups={{0,64,16,80},{32,96,48,112},{128,192,144,208},{160,224,176,240},{256,32..., dimensions={0} | all-to-all | bytes 3145728 | tf_op jit(solution)/shard_map/all_to_all | solution.py:46
  54.9 1.9 %partial_sums.1 = (f32[2,128,384]{2,1,0:T(8,128)S(1)}, f32[2,128,384]{2,1,0:T(8,128)S(1)}, bf16[4,2,64,1536]{3,2,1,0:T(8,128)(2,1)S(1)}) custom-call(s32[1]{0:T(128)} %bitcast.2.core_ref, s32[12,3]{1,0:T(8,128)S(1)} %dynamic_slice.5.mask_ref, bf16[4,2,64,1536]{3,2,1,0:T(8,128)(2,1)S(1)} %all_to_all.30.near_ref, bf16[1536,384]{1,0:T(8,128)(2,1)S(1)} %copy-done, ...), custom_call_target="tpu_custom_call" | custom-call | flops 603979776 | bytes 3932160 | tf_op jit(solution)/shard_map/partial_sums/pallas_call | solution.py:166
  56.8 1.2 copy-done.2
  57.9 2.9 %collective-permute-start = (f32[2,128,384]{2,1,0:T(8,128)S(1)}, f32[2,128,384]{2,1,0:T(8,128)S(1)}, u32[]{:S(2)}, u32[]{:S(2)}) collective-permute-start(f32[2,128,384]{2,1,0:T(8,128)S(1)} %get-tuple-element.25), channel_id=1, source_target_pairs={{0,1},{1,0},{2,3},{3,2},{4,5},{5,4},{6,7},{7,6},{8,9},{9,8},{10,11... | collective-permute-start | bytes 1179656 | tf_op jit(solution)/shard_map/ppermute | solution.py:177
  60.9 1.3 %collective-permute-done = f32[2,128,384]{2,1,0:T(8,128)S(1)} collective-permute-done((f32[2,128,384]{2,1,0:T(8,128)S(1)}, f32[2,128,384]{2,1,0:T(8,128)S(1)}, u32[]{:S(2)}, u32[]{:S(2)}) %collective-permute-start) | collective-permute-done | bytes 393248 | tf_op jit(solution)/shard_map/ppermute | solution.py:177
  62.3 9.5 %all_to_all.31 = bf16[4,2,32,384]{3,2,1,0:T(8,128)(2,1)S(1)} all-to-all(bf16[4,2,32,384]{3,2,1,0:T(8,128)(2,1)S(1)} %bitcast.30), channel_id=1, replica_groups=mesh['zh'=4,'zl'=2,'xh'=2,'xl'=2,'yh'=2,'ylh'=2,'yll'=2,'core'=2] {'yll'..., dimensions={0} | all-to-all | bytes 393216 | tf_op jit(solution)/shard_map/all_to_all | solution.py:57
  71.9 9.5 %all_to_all.32 = bf16[4,2,32,384]{3,2,1,0:T(8,128)(2,1)S(1)} all-to-all(bf16[4,2,32,384]{3,2,1,0:T(8,128)(2,1)S(1)} %broadcast_in_dim.22), channel_id=1, replica_groups=mesh['zh'=4,'zl'=2,'xh'=2,'xl'=2,'yh'=2,'ylh'=2,'yll'=2,'core'=2] {'yll'..., dimensions={0} | all-to-all | bytes 393216 | tf_op jit(solution)/shard_map/all_to_all | solution.py:53
  81.4 2.1 %all_gather.3 = bf16[2,256,384]{2,1,0:T(8,128)(2,1)S(1)} all-gather(bf16[1,256,384]{2,1,0:T(8,128)(2,1)S(1)} %bitcast.31), channel_id=1, replica_groups=mesh['zh'=4,'zl'=2,'xh'=2,'xl'=2,'yh'=2,'ylh'=2,'yll'=2,'core'=2] {'core'}, dimensions={0}, use_global_device_ids=true | all-gather | bytes 589824 | tf_op jit(solution)/shard_map/all_gather | solution.py:187
  83.5 1.7 %output_terms.1 = bf16[4,2,64,1536]{3,2,1,0:T(8,128)(2,1)S(1)} custom-call(s32[12,3]{1,0:T(8,128)S(1)} %dynamic_slice.5.mask_ref, bf16[8,2,32,384]{3,2,1,0:T(8,128)(2,1)S(1)} %bitcast.23, bf16[1536,384]{1,0:T(8,128)(2,1)S(1)} %copy-done, bf16[384,1536]{1,0:T(8,128)(2,1)S(1)} %copy-done.1), custom_call_target="tpu_custom_call" | custom-call | flops 603979776 | bytes 3932160 | tf_op jit(solution)/shard_map/output_terms/pallas_call | solution.py:189
  85.2 15.2 %all_to_all.33 = bf16[4,2,64,1536]{3,2,1,0:T(8,128)(2,1)S(1)} all-to-all(bf16[4,2,64,1536]{3,2,1,0:T(8,128)(2,1)S(1)} %output_terms.1), channel_id=1, replica_groups={{0,64,16,80},{32,96,48,112},{128,192,144,208},{160,224,176,240},{256,32..., dimensions={0} | all-to-all | bytes 3145728 | tf_op jit(solution)/shard_map/all_to_all | solution.py:46
  100.4 0.3 reduce_sum.34
  100.7 0.4 copy.17
  101.1 0.9 copy.18
  102.0 6.5 %all-to-all-start.5 = ((bf16[16,2,4,1536]{3,2,1,0:T(4,128)(2,1)}), bf16[16,2,4,1536]{3,2,1,0:T(4,128)(2,1)S(1)}, u32[]{:S(2)}, u32[]{:S(2)}) async-start(bf16[16,2,4,1536]{3,2,1,0:T(4,128)(2,1)} %copy.18), calls=%async_computation.5 | async-start | bytes 786432 | tf_op jit(solution)/shard_map/all_to_all | solution.py:57
  108.5 2.8 %weight_grads.1 = (bf16[1536,384]{1,0:T(8,128)(2,1)}, bf16[384,1536]{1,0:T(8,128)(2,1)}) custom-call(s32[12,3]{1,0:T(8,128)S(1)} %dynamic_slice.5.mask_ref, bf16[8,2,32,384]{3,2,1,0:T(8,128)(2,1)S(1)} %bitcast.24, bf16[4,2,64,1536]{3,2,1,0:T(8,128)(2,1)S(1)} %copy-done.3), custom_call_target="tpu_custom_call" | custom-call | flops 603979776 | bytes 3932160 | tf_op jit(solution)/shard_map/weight_grads/pallas_call | solution.py:206
  111.4 17.7 %all-to-all-done.5 = bf16[16,2,4,1536]{3,2,1,0:T(4,128)(2,1)S(1)} async-done(((bf16[16,2,4,1536]{3,2,1,0:T(4,128)(2,1)}), bf16[16,2,4,1536]{3,2,1,0:T(4,128)(2,1)S(1)}, u32[]{:S(2)}, u32[]{:S(2)}) %all-to-all-start.5) | async-done | bytes 393248 | tf_op jit(solution)/shard_map/all_to_all | solution.py:57
  129.1 0.2 reduce_sum.35
  129.2 0.6 slice_bitcast_fusion
  (17 shorter events, 0.4 us)
Async XLA Ops:
  2.2 36.8 %all-to-all-start = ((bf16[16,2,4,1536]{3,2,1,0:T(4,128)(2,1)}), bf16[16,2,4,1536]{3,2,1,0:T(4,128)(2,1)S(1)}, u32[]{:S(2)}, u32[]{:S(2)}) async-start(bf16[16,2,4,1536]{3,2,1,0:T(4,128)(2,1)} %broadcast_in_dim.8), calls=%async_computation | async-start | bytes 786432 | tf_op jit(solution)/shard_map/all_to_all | solution.py:53
  39.5 15.4 %copy-start = (bf16[1536,384]{1,0:T(8,128)(2,1)S(1)}, bf16[1536,384]{1,0:T(8,128)(2,1)}, u32[]{:S(2)}) copy-start(bf16[1536,384]{1,0:T(8,128)(2,1)} %up_ref.3) | copy-start | bytes 3538948
  39.5 15.3 %copy-start.1 = (bf16[384,1536]{1,0:T(8,128)(2,1)S(1)}, bf16[384,1536]{1,0:T(8,128)(2,1)}, u32[]{:S(2)}) copy-start(bf16[384,1536]{1,0:T(8,128)(2,1)} %down_ref.3) | copy-start | bytes 3538948
  56.8 1.2 copy-start.2
  57.9 4.3 %collective-permute-start = (f32[2,128,384]{2,1,0:T(8,128)S(1)}, f32[2,128,384]{2,1,0:T(8,128)S(1)}, u32[]{:S(2)}, u32[]{:S(2)}) collective-permute-start(f32[2,128,384]{2,1,0:T(8,128)S(1)} %get-tuple-element.25), channel_id=1, source_target_pairs={{0,1},{1,0},{2,3},{3,2},{4,5},{5,4},{6,7},{7,6},{8,9},{9,8},{10,11... | collective-permute-start | bytes 1179656 | tf_op jit(solution)/shard_map/ppermute | solution.py:177
  100.7 7.8 %copy-start.3 = (bf16[4,2,64,1536]{3,2,1,0:T(8,128)(2,1)S(1)}, bf16[4,2,64,1536]{3,2,1,0:T(8,128)(2,1)}, u32[]{:S(2)}) copy-start(bf16[4,2,64,1536]{3,2,1,0:T(8,128)(2,1)} %copy-done.2) | copy-start | bytes 4718596
  102.0 27.0 %all-to-all-start.5 = ((bf16[16,2,4,1536]{3,2,1,0:T(4,128)(2,1)}), bf16[16,2,4,1536]{3,2,1,0:T(4,128)(2,1)S(1)}, u32[]{:S(2)}, u32[]{:S(2)}) async-start(bf16[16,2,4,1536]{3,2,1,0:T(4,128)(2,1)} %copy.18), calls=%async_computation.5 | async-start | bytes 786432 | tf_op jit(solution)/shard_map/all_to_all | solution.py:57

commit v5 on v4

--- a/solution.py
+++ b/solution.py
@@ -17,7 +17,8 @@
 FARS = 16
 NEARS = 4
 LINE = ("yll", "ylh")
-VMEM_BYTES = 10 * 1024 * 1024
+VMEM_BYTES = 12 * 1024 * 1024
+LARGE_VMEM_BYTES = 56 * 1024 * 1024
 
 slope_coef = 0.7978845608
 cubic_coef = 0.044715
@@ -77,21 +78,18 @@
 
 
 def first_kernel(
-    core_ref, mask_ref, near_ref, up_ref, down_ref, keep_ref, give_ref, saved_ref, um, dm, sem
+    core_ref, mask_ref, near_ref, up_ref, down_ref, keep_ref, give_ref, um, dm
 ):
-    saving = pltpu.make_async_copy(near_ref, saved_ref, sem)
-    saving.start()
     mask_weights(mask_ref, up_ref, down_ref, um, dm)
     width = um.shape[0]
     half = keep_ref.shape[1]
-    hidden = dot(near_ref[:, 0].reshape(2 * half, width), um[...], 1, 0)
-    grad = dot(near_ref[:, 1].reshape(2 * half, width), dm[...], 1, 1)
+    hidden = dot(near_ref[:, :, :width].reshape(2 * half, width), um[...], 1, 0)
+    grad = dot(near_ref[:, :, width:].reshape(2 * half, width), dm[...], 1, 1)
     low = core_ref[0] == 0
     for k, part in enumerate((hidden, grad)):
         a, b = part[:half], part[half:]
         keep_ref[k] = jnp.where(low, a, b)
         give_ref[k] = jnp.where(low, b, a)
-    saving.wait()
 
 
 def second_kernel(mask_ref, acts_ref, up_ref, down_ref, terms_ref, um, dm):
@@ -101,16 +99,24 @@
     wide = width // 3
     act = acts_ref[:, 0].reshape(blocks * rows, units)
     dact = acts_ref[:, 1].reshape(blocks * rows, units)
-    blocks, _, rows, _ = terms_ref.shape
+    blocks, rows, _ = terms_ref.shape
     for k in range(3):
         w = slice(k * wide, (k + 1) * wide)
         out = dot(act, dm[:, w], 1, 0).astype(terms_ref.dtype)
-        terms_ref[:, 0, :, w] = out.reshape(blocks, rows, wide)
+        terms_ref[:, :, w] = out.reshape(blocks, rows, wide)
         back = dot(dact, um[w, :], 1, 1).astype(terms_ref.dtype)
-        terms_ref[:, 1, :, w] = back.reshape(blocks, rows, wide)
-
-
-def third_kernel(mask_ref, acts_ref, near_ref, upg_ref, downg_ref):
+        terms_ref[:, :, width + k * wide : width + (k + 1) * wide] = back.reshape(blocks, rows, wide)
+
+
+def third_kernel(mask_ref, acts_ref, saved_ref, upg_ref, downg_ref, near_ref, sem):
+    loading = [
+        pltpu.make_async_copy(saved_ref.at[i], near_ref.at[i], sem.at[i])
+        for i in range(near_ref.shape[0])
+    ]
+    for copy in loading:
+        copy.start()
+    for copy in loading:
+        copy.wait()
     blocks, _, rows, units = acts_ref.shape
     width = upg_ref.shape[0]
     wide = width // 3
@@ -119,8 +125,9 @@
     dact = acts_ref[:, 1].reshape(tokens, units)
     for k in range(3):
         w = slice(k * wide, (k + 1) * wide)
-        down = dot(act, near_ref[:, 1, :, w].reshape(tokens, wide), 0, 0).astype(downg_ref.dtype)
-        up = dot(near_ref[:, 0, :, w].reshape(tokens, wide), dact, 0, 0).astype(upg_ref.dtype)
+        g = near_ref[:, :, width + k * wide : width + (k + 1) * wide].reshape(tokens, wide)
+        down = dot(act, g, 0, 0).astype(downg_ref.dtype)
+        up = dot(near_ref[:, :, w].reshape(tokens, wide), dact, 0, 0).astype(upg_ref.dtype)
         for i in range(wide // BLK):
             d = slice(i * BLK, (i + 1) * BLK)
             at = slice(k * wide + i * BLK, k * wide + (i + 1) * BLK)
@@ -145,6 +152,7 @@
     bf, f4 = jnp.bfloat16, jnp.float32
     smem = pl.BlockSpec(memory_space=pltpu.SMEM)
     vmem = pl.BlockSpec(memory_space=pltpu.VMEM)
+    hbm = pl.BlockSpec(memory_space=pltpu.HBM)
     params = pltpu.CompilerParams(vmem_limit_bytes=VMEM_BYTES)
     cost = pl.CostEstimate(
         flops=4 * tokens * width * units,
@@ -154,22 +162,21 @@
     scratch = [pltpu.VMEM((width, units), bf), pltpu.VMEM((units, width), bf)]
     masked = [jax.ShapeDtypeStruct((width, units), bf), jax.ShapeDtypeStruct((units, width), bf)]
 
-    both = jnp.stack([inputs, out_grad])
+    both = jnp.concatenate([inputs, out_grad], axis=1)
     far = spread(both, FAR, FARS)
     mask = lax.dynamic_slice(
         block_mask, (col_index * d_blocks, row_index * f_blocks), (d_blocks, f_blocks)
     )
     far, mask = lax.optimization_barrier((far, mask))
-    far = far.transpose(1, 0, 2, 3).reshape(1, 2, FARS * rows, width)
+    far = far.reshape(1, FARS * rows, 2 * width)
     near = near_swap(jnp.broadcast_to(far, (NEARS,) + far.shape[1:]))
 
-    keep, give, saved = pl.pallas_call(
+    keep, give = pl.pallas_call(
         first_kernel,
         in_specs=[smem, smem, vmem, vmem, vmem],
-        out_specs=[vmem, vmem, pl.BlockSpec(memory_space=pltpu.HBM)],
-        out_shape=[jax.ShapeDtypeStruct((2, half, units), f4)] * 2
-        + [jax.ShapeDtypeStruct(near.shape, bf)],
-        scratch_shapes=scratch + [pltpu.SemaphoreType.DMA],
+        out_specs=[vmem, vmem],
+        out_shape=[jax.ShapeDtypeStruct((2, half, units), f4)] * 2,
+        scratch_shapes=scratch,
         compiler_params=params,
         cost_estimate=cost,
         name="partial_sums",
@@ -190,7 +197,7 @@
         second_kernel,
         in_specs=[smem, vmem, vmem, vmem],
         out_specs=vmem,
-        out_shape=jax.ShapeDtypeStruct((NEARS, 2, FARS * rows, width), bf),
+        out_shape=jax.ShapeDtypeStruct((NEARS, FARS * rows, 2 * width), bf),
         scratch_shapes=scratch,
         compiler_params=params,
         cost_estimate=cost,
@@ -198,23 +205,24 @@
     )(mask, acts, up_weight, down_weight)
 
     terms = near_swap(terms)
-    terms, acts, saved = lax.optimization_barrier((terms, acts, saved))
+    terms, acts, near = lax.optimization_barrier((terms, acts, near))
     sums = jnp.sum(terms.astype(f4), axis=0).astype(bf)
-    sums = sums.reshape(2, FARS, rows, width).transpose(1, 0, 2, 3)
-    sums, acts, saved = lax.optimization_barrier((sums, acts, saved))
+    sums = sums.reshape(FARS, rows, 2 * width)
+    sums, acts, near = lax.optimization_barrier((sums, acts, near))
     sums = swap(sums, FAR)
     up_grad, down_grad = pl.pallas_call(
         third_kernel,
-        in_specs=[smem, vmem, vmem],
+        in_specs=[smem, vmem, hbm],
         out_specs=[vmem, vmem],
         out_shape=masked,
-        compiler_params=params,
+        scratch_shapes=[pltpu.VMEM(near.shape, bf), pltpu.SemaphoreType.DMA((NEARS,))],
+        compiler_params=pltpu.CompilerParams(vmem_limit_bytes=LARGE_VMEM_BYTES),
         cost_estimate=cost,
         name="weight_grads",
-    )(mask, acts, saved)
+    )(mask, acts, near)
     sums, up_grad, down_grad = lax.optimization_barrier((sums, up_grad, down_grad))
     totals = jnp.sum(sums.astype(f4), axis=0).astype(bf)
-    return (totals[0], totals[1], up_grad, down_grad)
+    return (totals[:, :width], totals[:, width:], up_grad, down_grad)
 
 
 def solution(mesh):

time: 130 us -> 129 us (level)
  local copies, waits for them, and re-layouts: 5.28 us -> 3.53 us
  waiting for transfers between devices: 37.7 us -> 36 us
  Pallas kernels: 6.47 us -> 8.03 us
    pallas_call x1, Pallas kernels: 2.85 us -> 4.57 us  [local(): pl.pallas_call(third_kernel, in_specs=[smem, vmem, hbm], out_specs=[vmem,...]
    all_to_all x1, waiting for transfers between devices: 17.7 us -> 16 us  [swap(): return lax.all_to_all(blocks, axes, split_axis=0, concat_axis=0, tiled=True)]
  transfers between devices with their start and end apart: 3 -> 3, of which waited for: 3 -> 3; matrix products, arithmetic and copies ran while one was open for 1% -> 1% of each run, Pallas kernels for 2% -> 4%
where the time goes in v5:
time: 129 us; the launch traced here: 128 us
  blocking collectives  51.7 us (40%)
  waiting for transfers between devices  36 us (28%)
  starting transfers between devices  26.7 us (21%)
  Pallas kernels  8.03 us (6%)
  local copies, waits for them, and re-layouts  3.53 us (3%)
  other arithmetic  1.39 us (1%)
    all_to_all x2, blocking collectives, near_swap(): lax.all_to_all(blocks, AXES, split_axis=0, concat_axis=0, tiled=True, axi...  30.5 us
    all_to_all x1, waiting for transfers between devices, spread(): return lax.all_to_all(copies, axes, split_axis=0, concat_axis=0, tiled=True)  18.7 us
    all_to_all x1, starting transfers between devices, spread(): return lax.all_to_all(copies, axes, split_axis=0, concat_axis=0, tiled=True)  17.2 us
    all_to_all x1, waiting for transfers between devices, swap(): return lax.all_to_all(blocks, axes, split_axis=0, concat_axis=0, tiled=True)  16 us
    all_to_all x1, blocking collectives, swap(): return lax.all_to_all(blocks, axes, split_axis=0, concat_axis=0, tiled=True)  9.6 us
    all_to_all x1, blocking collectives, spread(): return lax.all_to_all(copies, axes, split_axis=0, concat_axis=0, tiled=True)  9.52 us
    all_to_all x1, starting transfers between devices, swap(): return lax.all_to_all(blocks, axes, split_axis=0, concat_axis=0, tiled=True)  6.5 us
    pallas_call x1, Pallas kernels, local(): pl.pallas_call(third_kernel, in_specs=[smem, vmem, hbm], out_specs=[vmem,...  4.57 us
  transfers between devices with their start and end apart: 3, of which 3 were waited for; matrix products, arithmetic and copies ran while one was open for 1% of the time, Pallas kernels for 4%

profile of v5, /device:TPU:8, one launch (start us, length us, event | category | flops | bytes accessed | tf_op | source)
XLA Modules:
  0.0 128.1 jit_solution(15924788159808162707)
XLA Ops:
  0.6 0.7 pad_maximum_fusion.1
  1.4 0.8 broadcast_in_dim.8
  2.2 17.2 %all-to-all-start = ((bf16[16,4,3072]{2,1,0:T(4,128)(2,1)}), bf16[16,4,3072]{2,1,0:T(4,128)(2,1)S(1)}, u32[]{:S(2)}, u32[]{:S(2)}) async-start(bf16[16,4,3072]{2,1,0:T(4,128)(2,1)} %broadcast_in_dim.8), calls=%async_computation | async-start | bytes 786432 | tf_op jit(solution)/shard_map/all_to_all | solution.py:54
  19.5 0.8 dynamic_slice.5.mask_ref
  20.3 18.7 %all-to-all-done = bf16[16,4,3072]{2,1,0:T(4,128)(2,1)S(1)} async-done(((bf16[16,4,3072]{2,1,0:T(4,128)(2,1)}), bf16[16,4,3072]{2,1,0:T(4,128)(2,1)S(1)}, u32[]{:S(2)}, u32[]{:S(2)}) %all-to-all-start) | async-done | bytes 393248 | tf_op jit(solution)/shard_map/all_to_all | solution.py:54
  39.0 0.1 broadcast_in_dim.9
  39.1 0.2 broadcast_in_dim.10
  39.3 0.0 copy-start.1
  39.3 15.3 %all_to_all.30.near_ref.saved_ref = bf16[4,64,3072]{2,1,0:T(8,128)(2,1)S(1)} all-to-all(bf16[4,64,3072]{2,1,0:T(8,128)(2,1)S(1)} %broadcast_in_dim.10), channel_id=1, replica_groups={{0,64,16,80},{32,96,48,112},{128,192,144,208},{160,224,176,240},{256,32..., dimensions={0} | all-to-all | bytes 3145728 | tf_op jit(solution)/shard_map/all_to_all | solution.py:47
  54.6 1.7 %partial_sums.1 = (f32[2,128,384]{2,1,0:T(8,128)S(1)}, f32[2,128,384]{2,1,0:T(8,128)S(1)}) custom-call(s32[1]{0:T(128)} %bitcast.core_ref, s32[12,3]{1,0:T(8,128)S(1)} %dynamic_slice.5.mask_ref, bf16[4,64,3072]{2,1,0:T(8,128)(2,1)S(1)} %all_to_all.30.near_ref.saved_ref, bf16[1536,384]{1,0:T(8,128)(2,1)S(1)} %copy-done.1, bf16[384,1536]{1,0:T(8,128)(2,1)S(1)} %copy-done.2), custom_call_target="tpu_custom_call" | custom-call | flops 603979776 | bytes 3932160 | tf_op jit(solution)/shard_map/partial_sums/pallas_call | solution.py:174
  56.4 2.9 %collective-permute-start = (f32[2,128,384]{2,1,0:T(8,128)S(1)}, f32[2,128,384]{2,1,0:T(8,128)S(1)}, u32[]{:S(2)}, u32[]{:S(2)}) collective-permute-start(f32[2,128,384]{2,1,0:T(8,128)S(1)} %get-tuple-element.24), channel_id=1, source_target_pairs={{0,1},{1,0},{2,3},{3,2},{4,5},{5,4},{6,7},{7,6},{8,9},{9,8},{10,11... | collective-permute-start | bytes 1179656 | tf_op jit(solution)/shard_map/ppermute | solution.py:184
  59.3 1.3 %collective-permute-done = f32[2,128,384]{2,1,0:T(8,128)S(1)} collective-permute-done((f32[2,128,384]{2,1,0:T(8,128)S(1)}, f32[2,128,384]{2,1,0:T(8,128)S(1)}, u32[]{:S(2)}, u32[]{:S(2)}) %collective-permute-start) | collective-permute-done | bytes 393248 | tf_op jit(solution)/shard_map/ppermute | solution.py:184
  60.8 9.6 %all_to_all.31 = bf16[4,2,32,384]{3,2,1,0:T(8,128)(2,1)S(1)} all-to-all(bf16[4,2,32,384]{3,2,1,0:T(8,128)(2,1)S(1)} %bitcast.16), channel_id=1, replica_groups=mesh['zh'=4,'zl'=2,'xh'=2,'xl'=2,'yh'=2,'ylh'=2,'yll'=2,'core'=2] {'yll'..., dimensions={0} | all-to-all | bytes 393216 | tf_op jit(solution)/shard_map/all_to_all | solution.py:58
  70.5 9.5 %all_to_all.32 = bf16[4,2,32,384]{3,2,1,0:T(8,128)(2,1)S(1)} all-to-all(bf16[4,2,32,384]{3,2,1,0:T(8,128)(2,1)S(1)} %broadcast_in_dim.22), channel_id=1, replica_groups=mesh['zh'=4,'zl'=2,'xh'=2,'xl'=2,'yh'=2,'ylh'=2,'yll'=2,'core'=2] {'yll'..., dimensions={0} | all-to-all | bytes 393216 | tf_op jit(solution)/shard_map/all_to_all | solution.py:54
  80.0 2.1 %all_gather.3 = bf16[2,256,384]{2,1,0:T(8,128)(2,1)S(1)} all-gather(bf16[1,256,384]{2,1,0:T(8,128)(2,1)S(1)} %bitcast.17), channel_id=1, replica_groups=mesh['zh'=4,'zl'=2,'xh'=2,'xl'=2,'yh'=2,'ylh'=2,'yll'=2,'core'=2] {'core'}, dimensions={0}, use_global_device_ids=true | all-gather | bytes 589824 | tf_op jit(solution)/shard_map/all_gather | solution.py:194
  82.1 1.7 %output_terms.1 = bf16[4,64,3072]{2,1,0:T(8,128)(2,1)S(1)} custom-call(s32[12,3]{1,0:T(8,128)S(1)} %dynamic_slice.5.mask_ref, bf16[8,2,32,384]{3,2,1,0:T(8,128)(2,1)S(1)} %bitcast.12, bf16[1536,384]{1,0:T(8,128)(2,1)S(1)} %copy-done.1, bf16[384,1536]{1,0:T(8,128)(2,1)S(1)} %copy-done.3), custom_call_target="tpu_custom_call" | custom-call | flops 603979776 | bytes 3932160 | tf_op jit(solution)/shard_map/output_terms/pallas_call | solution.py:196
  83.9 15.2 %all_to_all.33 = bf16[4,64,3072]{2,1,0:T(8,128)(2,1)S(1)} all-to-all(bf16[4,64,3072]{2,1,0:T(8,128)(2,1)S(1)} %output_terms.1), channel_id=1, replica_groups={{0,64,16,80},{32,96,48,112},{128,192,144,208},{160,224,176,240},{256,32..., dimensions={0} | all-to-all | bytes 3145728 | tf_op jit(solution)/shard_map/all_to_all | solution.py:47
  99.1 0.3 reduce_sum.34
  99.4 0.9 reshape.47
  100.3 6.5 %all-to-all-start.5 = ((bf16[16,4,3072]{2,1,0:T(4,128)(2,1)}), bf16[16,4,3072]{2,1,0:T(4,128)(2,1)S(1)}, u32[]{:S(2)}, u32[]{:S(2)}) async-start(bf16[16,4,3072]{2,1,0:T(4,128)(2,1)} %reshape.47), calls=%async_computation.5 | async-start | bytes 786432 | tf_op jit(solution)/shard_map/all_to_all | solution.py:58
  106.8 4.6 %weight_grads.1 = (bf16[1536,384]{1,0:T(8,128)(2,1)}, bf16[384,1536]{1,0:T(8,128)(2,1)}) custom-call(s32[12,3]{1,0:T(8,128)} %copy-done.5, bf16[8,2,32,384]{3,2,1,0:T(8,128)(2,1)} %bitcast.13, bf16[4,64,3072]{2,1,0:T(8,128)(2,1)} %copy-done), custom_call_target="tpu_custom_call" | custom-call | flops 603979776 | bytes 3932160 | tf_op jit(solution)/shard_map/weight_grads/pallas_call | solution.py:213
  111.4 16.0 %all-to-all-done.5 = bf16[16,4,3072]{2,1,0:T(4,128)(2,1)S(1)} async-done(((bf16[16,4,3072]{2,1,0:T(4,128)(2,1)}), bf16[16,4,3072]{2,1,0:T(4,128)(2,1)S(1)}, u32[]{:S(2)}, u32[]{:S(2)}) %all-to-all-start.5) | async-done | bytes 393248 | tf_op jit(solution)/shard_map/all_to_all | solution.py:58
  127.3 0.2 reduce_sum.35
  127.5 0.6 fusion.8
  (19 shorter events, 0.2 us)
Async XLA Ops:
  2.2 36.8 %all-to-all-start = ((bf16[16,4,3072]{2,1,0:T(4,128)(2,1)}), bf16[16,4,3072]{2,1,0:T(4,128)(2,1)S(1)}, u32[]{:S(2)}, u32[]{:S(2)}) async-start(bf16[16,4,3072]{2,1,0:T(4,128)(2,1)} %broadcast_in_dim.8), calls=%async_computation | async-start | bytes 786432 | tf_op jit(solution)/shard_map/all_to_all | solution.py:54
  20.3 61.8 %copy-start.5 = (s32[12,3]{1,0:T(8,128)}, s32[12,3]{1,0:T(8,128)S(1)}, u32[]{:S(2)}) copy-start(s32[12,3]{1,0:T(8,128)S(1)} %dynamic_slice.5.mask_ref) | copy-start | bytes 436
  39.3 15.4 %copy-start.1 = (bf16[1536,384]{1,0:T(8,128)(2,1)S(1)}, bf16[1536,384]{1,0:T(8,128)(2,1)}, u32[]{:S(2)}) copy-start(bf16[1536,384]{1,0:T(8,128)(2,1)} %up_ref.3) | copy-start | bytes 3538948
  39.3 15.3 %copy-start.2 = (bf16[384,1536]{1,0:T(8,128)(2,1)S(1)}, bf16[384,1536]{1,0:T(8,128)(2,1)}, u32[]{:S(2)}) copy-start(bf16[384,1536]{1,0:T(8,128)(2,1)} %down_ref.3) | copy-start | bytes 3538948
  54.6 1.7 %copy-start = (bf16[4,64,3072]{2,1,0:T(8,128)(2,1)}, bf16[4,64,3072]{2,1,0:T(8,128)(2,1)S(1)}, u32[]{:S(2)}) copy-start(bf16[4,64,3072]{2,1,0:T(8,128)(2,1)S(1)} %all_to_all.30.near_ref.saved_ref) | copy-start | bytes 4718596
  56.4 4.3 %collective-permute-start = (f32[2,128,384]{2,1,0:T(8,128)S(1)}, f32[2,128,384]{2,1,0:T(8,128)S(1)}, u32[]{:S(2)}, u32[]{:S(2)}) collective-permute-start(f32[2,128,384]{2,1,0:T(8,128)S(1)} %get-tuple-element.24), channel_id=1, source_target_pairs={{0,1},{1,0},{2,3},{3,2},{4,5},{5,4},{6,7},{7,6},{8,9},{9,8},{10,11... | collective-permute-start | bytes 1179656 | tf_op jit(solution)/shard_map/ppermute | solution.py:184
  60.7 21.4 %copy-start.3 = (bf16[384,1536]{1,0:T(8,128)(2,1)S(1)}, bf16[384,1536]{1,0:T(8,128)(2,1)}, u32[]{:S(2)}) copy-start(bf16[384,1536]{1,0:T(8,128)(2,1)} %down_ref.3) | copy-start | bytes 3538948
  82.1 1.7 %copy-start.4 = (bf16[2,256,384]{2,1,0:T(8,128)(2,1)}, bf16[2,256,384]{2,1,0:T(8,128)(2,1)S(1)}, u32[]{:S(2)}) copy-start(bf16[2,256,384]{2,1,0:T(8,128)(2,1)S(1)} %all_gather.3) | copy-start | bytes 1179652
  100.3 27.0 %all-to-all-start.5 = ((bf16[16,4,3072]{2,1,0:T(4,128)(2,1)}), bf16[16,4,3072]{2,1,0:T(4,128)(2,1)S(1)}, u32[]{:S(2)}, u32[]{:S(2)}) async-start(bf16[16,4,3072]{2,1,0:T(4,128)(2,1)} %reshape.47), calls=%async_computation.5 | async-start | bytes 786432 | tf_op jit(solution)/shard_map/all_to_all | solution.py:58

commit v6 on v5

--- a/solution.py
+++ b/solution.py
@@ -183,11 +183,7 @@
     )(core.reshape(1), mask, near, up_weight, down_weight)
     pair = keep + lax.ppermute(give, "core", [(0, 1), (1, 0)])
     pair = pair.reshape(2, 4, quarter, units).transpose(1, 0, 2, 3)
-    sent = pair.astype(bf)
-    lost = lax.dynamic_index_in_dim(pair, lax.axis_index(LINE), 0, keepdims=False)
-    lost = lost - lost.astype(bf).astype(f4)
-    sent, lost = lax.optimization_barrier((sent, lost))
-    summed = jnp.sum(swap(sent, LINE).astype(f4), axis=0) + lost
+    summed = jnp.sum(swap(pair, LINE), axis=0)
     value, slope = gelu_pair(summed[0])
     acts = jnp.stack([value, summed[1] * slope]).astype(bf)
     acts = spread(acts, LINE, 4).reshape(1, 8 * quarter, units)

time: 129 us -> 133 us (1.031)
  blocking collectives: 51.7 us -> 55.9 us
    all_to_all x1, blocking collectives: 9.6 us -> 13.6 us  [swap(): return lax.all_to_all(blocks, axes, split_axis=0, concat_axis=0, tiled=True)]
  transfers between devices with their start and end apart: 3 -> 3, of which waited for: 3 -> 3; matrix products, arithmetic and copies ran while one was open for 1% -> 1% of each run, Pallas kernels for 4% -> 3%
where the time goes in v6:
time: 133 us; the launch traced here: 132 us
  blocking collectives  55.9 us (42%)
  waiting for transfers between devices  35.9 us (27%)
  starting transfers between devices  26.7 us (20%)
  Pallas kernels  8.02 us (6%)
  local copies, waits for them, and re-layouts  3.54 us (3%)
  other arithmetic  1.37 us (1%)
    all_to_all x2, blocking collectives, near_swap(): lax.all_to_all(blocks, AXES, split_axis=0, concat_axis=0, tiled=True, axi...  30.5 us
    all_to_all x1, waiting for transfers between devices, spread(): return lax.all_to_all(copies, axes, split_axis=0, concat_axis=0, tiled=True)  18.7 us
    all_to_all x1, starting transfers between devices, spread(): return lax.all_to_all(copies, axes, split_axis=0, concat_axis=0, tiled=True)  17.2 us
    all_to_all x1, waiting for transfers between devices, swap(): return lax.all_to_all(blocks, axes, split_axis=0, concat_axis=0, tiled=True)  15.9 us
    all_to_all x1, blocking collectives, swap(): return lax.all_to_all(blocks, axes, split_axis=0, concat_axis=0, tiled=True)  13.6 us
    all_to_all x1, blocking collectives, spread(): return lax.all_to_all(copies, axes, split_axis=0, concat_axis=0, tiled=True)  9.69 us
    all_to_all x1, starting transfers between devices, swap(): return lax.all_to_all(blocks, axes, split_axis=0, concat_axis=0, tiled=True)  6.54 us
    pallas_call x1, Pallas kernels, local(): pl.pallas_call(third_kernel, in_specs=[smem, vmem, hbm], out_specs=[vmem,...  4.57 us
  transfers between devices with their start and end apart: 3, of which 3 were waited for; matrix products, arithmetic and copies ran while one was open for 1% of the time, Pallas kernels for 3%

profile of v6, /device:TPU:8, one launch (start us, length us, event | category | flops | bytes accessed | tf_op | source)
XLA Modules:
  0.0 132.3 jit_solution(1381348325404712073)
XLA Ops:
  0.6 0.7 pad_maximum_fusion.1
  1.4 0.8 broadcast_in_dim.8
  2.2 17.2 %all-to-all-start = ((bf16[16,4,3072]{2,1,0:T(4,128)(2,1)}), bf16[16,4,3072]{2,1,0:T(4,128)(2,1)S(1)}, u32[]{:S(2)}, u32[]{:S(2)}) async-start(bf16[16,4,3072]{2,1,0:T(4,128)(2,1)} %broadcast_in_dim.8), calls=%async_computation | async-start | bytes 786432 | tf_op jit(solution)/shard_map/all_to_all | solution.py:54
  19.5 0.8 dynamic_slice.3.mask_ref
  20.3 18.7 %all-to-all-done = bf16[16,4,3072]{2,1,0:T(4,128)(2,1)S(1)} async-done(((bf16[16,4,3072]{2,1,0:T(4,128)(2,1)}), bf16[16,4,3072]{2,1,0:T(4,128)(2,1)S(1)}, u32[]{:S(2)}, u32[]{:S(2)}) %all-to-all-start) | async-done | bytes 393248 | tf_op jit(solution)/shard_map/all_to_all | solution.py:54
  39.0 0.1 broadcast_in_dim.9
  39.1 0.2 broadcast_in_dim.10
  39.3 15.3 %all_to_all.30.near_ref.saved_ref = bf16[4,64,3072]{2,1,0:T(8,128)(2,1)S(1)} all-to-all(bf16[4,64,3072]{2,1,0:T(8,128)(2,1)S(1)} %broadcast_in_dim.10), channel_id=1, replica_groups={{0,64,16,80},{32,96,48,112},{128,192,144,208},{160,224,176,240},{256,32..., dimensions={0} | all-to-all | bytes 3145728 | tf_op jit(solution)/shard_map/all_to_all | solution.py:47
  54.6 1.7 %partial_sums.1 = (f32[2,128,384]{2,1,0:T(8,128)S(1)}, f32[2,128,384]{2,1,0:T(8,128)S(1)}) custom-call(s32[1]{0:T(128)} %bitcast.core_ref, s32[12,3]{1,0:T(8,128)S(1)} %dynamic_slice.3.mask_ref, bf16[4,64,3072]{2,1,0:T(8,128)(2,1)S(1)} %all_to_all.30.near_ref.saved_ref, bf16[1536,384]{1,0:T(8,128)(2,1)S(1)} %copy-done.1, bf16[384,1536]{1,0:T(8,128)(2,1)S(1)} %copy-done.2), custom_call_target="tpu_custom_call" | custom-call | flops 603979776 | bytes 3932160 | tf_op jit(solution)/shard_map/partial_sums/pallas_call | solution.py:174
  56.4 2.9 %collective-permute-start = (f32[2,128,384]{2,1,0:T(8,128)S(1)}, f32[2,128,384]{2,1,0:T(8,128)S(1)}, u32[]{:S(2)}, u32[]{:S(2)}) collective-permute-start(f32[2,128,384]{2,1,0:T(8,128)S(1)} %get-tuple-element.22), channel_id=1, source_target_pairs={{0,1},{1,0},{2,3},{3,2},{4,5},{5,4},{6,7},{7,6},{8,9},{9,8},{10,11... | collective-permute-start | bytes 1179656 | tf_op jit(solution)/shard_map/ppermute | solution.py:184
  59.3 1.3 %collective-permute-done = f32[2,128,384]{2,1,0:T(8,128)S(1)} collective-permute-done((f32[2,128,384]{2,1,0:T(8,128)S(1)}, f32[2,128,384]{2,1,0:T(8,128)S(1)}, u32[]{:S(2)}, u32[]{:S(2)}) %collective-permute-start) | collective-permute-done | bytes 393248 | tf_op jit(solution)/shard_map/ppermute | solution.py:184
  60.7 0.1 add.54
  60.8 13.6 %all_to_all.31 = f32[4,2,32,384]{3,2,1,0:T(8,128)S(1)} all-to-all(f32[4,2,32,384]{3,2,1,0:T(8,128)S(1)} %bitcast.9), channel_id=1, replica_groups=mesh['zh'=4,'zl'=2,'xh'=2,'xl'=2,'yh'=2,'ylh'=2,'yll'=2,'core'=2] {'yll'..., dimensions={0} | all-to-all | bytes 786432 | tf_op jit(solution)/shard_map/all_to_all | solution.py:58
  74.5 9.7 %all_to_all.32 = bf16[4,2,32,384]{3,2,1,0:T(8,128)(2,1)S(1)} all-to-all(bf16[4,2,32,384]{3,2,1,0:T(8,128)(2,1)S(1)} %broadcast_in_dim.22), channel_id=1, replica_groups=mesh['zh'=4,'zl'=2,'xh'=2,'xl'=2,'yh'=2,'ylh'=2,'yll'=2,'core'=2] {'yll'..., dimensions={0} | all-to-all | bytes 393216 | tf_op jit(solution)/shard_map/all_to_all | solution.py:54
  84.2 2.1 %all_gather.3 = bf16[2,256,384]{2,1,0:T(8,128)(2,1)S(1)} all-gather(bf16[1,256,384]{2,1,0:T(8,128)(2,1)S(1)} %bitcast.11), channel_id=1, replica_groups=mesh['zh'=4,'zl'=2,'xh'=2,'xl'=2,'yh'=2,'ylh'=2,'yll'=2,'core'=2] {'core'}, dimensions={0}, use_global_device_ids=true | all-gather | bytes 589824 | tf_op jit(solution)/shard_map/all_gather | solution.py:190
  86.3 1.7 %output_terms.1 = bf16[4,64,3072]{2,1,0:T(8,128)(2,1)S(1)} custom-call(s32[12,3]{1,0:T(8,128)S(1)} %dynamic_slice.3.mask_ref, bf16[8,2,32,384]{3,2,1,0:T(8,128)(2,1)S(1)} %bitcast.7, bf16[1536,384]{1,0:T(8,128)(2,1)S(1)} %copy-done.1, bf16[384,1536]{1,0:T(8,128)(2,1)S(1)} %copy-done.3), custom_call_target="tpu_custom_call" | custom-call | flops 603979776 | bytes 3932160 | tf_op jit(solution)/shard_map/output_terms/pallas_call | solution.py:192
  88.0 15.2 %all_to_all.33 = bf16[4,64,3072]{2,1,0:T(8,128)(2,1)S(1)} all-to-all(bf16[4,64,3072]{2,1,0:T(8,128)(2,1)S(1)} %output_terms.1), channel_id=1, replica_groups={{0,64,16,80},{32,96,48,112},{128,192,144,208},{160,224,176,240},{256,32..., dimensions={0} | all-to-all | bytes 3145728 | tf_op jit(solution)/shard_map/all_to_all | solution.py:47
  103.2 0.3 reduce_sum.34
  103.6 0.9 reshape.45
  104.5 6.5 %all-to-all-start.5 = ((bf16[16,4,3072]{2,1,0:T(4,128)(2,1)}), bf16[16,4,3072]{2,1,0:T(4,128)(2,1)S(1)}, u32[]{:S(2)}, u32[]{:S(2)}) async-start(bf16[16,4,3072]{2,1,0:T(4,128)(2,1)} %reshape.45), calls=%async_computation.5 | async-start | bytes 786432 | tf_op jit(solution)/shard_map/all_to_all | solution.py:58
  111.0 4.6 %weight_grads.1 = (bf16[1536,384]{1,0:T(8,128)(2,1)}, bf16[384,1536]{1,0:T(8,128)(2,1)}) custom-call(s32[12,3]{1,0:T(8,128)} %copy-done.5, bf16[8,2,32,384]{3,2,1,0:T(8,128)(2,1)} %bitcast.8, bf16[4,64,3072]{2,1,0:T(8,128)(2,1)} %copy-done), custom_call_target="tpu_custom_call" | custom-call | flops 603979776 | bytes 3932160 | tf_op jit(solution)/shard_map/weight_grads/pallas_call | solution.py:209
  115.6 15.9 %all-to-all-done.5 = bf16[16,4,3072]{2,1,0:T(4,128)(2,1)S(1)} async-done(((bf16[16,4,3072]{2,1,0:T(4,128)(2,1)}), bf16[16,4,3072]{2,1,0:T(4,128)(2,1)S(1)}, u32[]{:S(2)}, u32[]{:S(2)}) %all-to-all-start.5) | async-done | bytes 393248 | tf_op jit(solution)/shard_map/all_to_all | solution.py:58
  131.5 0.2 reduce_sum.35
  131.7 0.6 fusion.7
  (17 shorter events, 0.2 us)
Async XLA Ops:
  2.2 36.8 %all-to-all-start = ((bf16[16,4,3072]{2,1,0:T(4,128)(2,1)}), bf16[16,4,3072]{2,1,0:T(4,128)(2,1)S(1)}, u32[]{:S(2)}, u32[]{:S(2)}) async-start(bf16[16,4,3072]{2,1,0:T(4,128)(2,1)} %broadcast_in_dim.8), calls=%async_computation | async-start | bytes 786432 | tf_op jit(solution)/shard_map/all_to_all | solution.py:54
  20.3 66.0 %copy-start.5 = (s32[12,3]{1,0:T(8,128)}, s32[12,3]{1,0:T(8,128)S(1)}, u32[]{:S(2)}) copy-start(s32[12,3]{1,0:T(8,128)S(1)} %dynamic_slice.3.mask_ref) | copy-start | bytes 436
  39.3 15.4 %copy-start.1 = (bf16[1536,384]{1,0:T(8,128)(2,1)S(1)}, bf16[1536,384]{1,0:T(8,128)(2,1)}, u32[]{:S(2)}) copy-start(bf16[1536,384]{1,0:T(8,128)(2,1)} %up_ref.3) | copy-start | bytes 3538948
  39.3 15.3 %copy-start.2 = (bf16[384,1536]{1,0:T(8,128)(2,1)S(1)}, bf16[384,1536]{1,0:T(8,128)(2,1)}, u32[]{:S(2)}) copy-start(bf16[384,1536]{1,0:T(8,128)(2,1)} %down_ref.3) | copy-start | bytes 3538948
  54.6 1.7 %copy-start = (bf16[4,64,3072]{2,1,0:T(8,128)(2,1)}, bf16[4,64,3072]{2,1,0:T(8,128)(2,1)S(1)}, u32[]{:S(2)}) copy-start(bf16[4,64,3072]{2,1,0:T(8,128)(2,1)S(1)} %all_to_all.30.near_ref.saved_ref) | copy-start | bytes 4718596
  56.4 4.3 %collective-permute-start = (f32[2,128,384]{2,1,0:T(8,128)S(1)}, f32[2,128,384]{2,1,0:T(8,128)S(1)}, u32[]{:S(2)}, u32[]{:S(2)}) collective-permute-start(f32[2,128,384]{2,1,0:T(8,128)S(1)} %get-tuple-element.22), channel_id=1, source_target_pairs={{0,1},{1,0},{2,3},{3,2},{4,5},{5,4},{6,7},{7,6},{8,9},{9,8},{10,11... | collective-permute-start | bytes 1179656 | tf_op jit(solution)/shard_map/ppermute | solution.py:184
  60.7 25.5 %copy-start.3 = (bf16[384,1536]{1,0:T(8,128)(2,1)S(1)}, bf16[384,1536]{1,0:T(8,128)(2,1)}, u32[]{:S(2)}) copy-start(bf16[384,1536]{1,0:T(8,128)(2,1)} %down_ref.3) | copy-start | bytes 3538948
  86.3 1.7 %copy-start.4 = (bf16[2,256,384]{2,1,0:T(8,128)(2,1)}, bf16[2,256,384]{2,1,0:T(8,128)(2,1)S(1)}, u32[]{:S(2)}) copy-start(bf16[2,256,384]{2,1,0:T(8,128)(2,1)S(1)} %all_gather.3) | copy-start | bytes 1179652
  104.5 27.0 %all-to-all-start.5 = ((bf16[16,4,3072]{2,1,0:T(4,128)(2,1)}), bf16[16,4,3072]{2,1,0:T(4,128)(2,1)S(1)}, u32[]{:S(2)}, u32[]{:S(2)}) async-start(bf16[16,4,3072]{2,1,0:T(4,128)(2,1)} %reshape.45), calls=%async_computation.5 | async-start | bytes 786432 | tf_op jit(solution)/shard_map/all_to_all | solution.py:58

commit v7 on v5

--- a/solution.py
+++ b/solution.py
@@ -77,19 +77,14 @@
             dm[f, d] = kept(mask_ref, i, j, down_ref[f, d])
 
 
-def first_kernel(
-    core_ref, mask_ref, near_ref, up_ref, down_ref, keep_ref, give_ref, um, dm
-):
+def first_kernel(half_ref, mask_ref, near_ref, up_ref, down_ref, part_ref, um, dm):
     mask_weights(mask_ref, up_ref, down_ref, um, dm)
     width = um.shape[0]
-    half = keep_ref.shape[1]
-    hidden = dot(near_ref[:, :, :width].reshape(2 * half, width), um[...], 1, 0)
-    grad = dot(near_ref[:, :, width:].reshape(2 * half, width), dm[...], 1, 1)
-    low = core_ref[0] == 0
-    for k, part in enumerate((hidden, grad)):
-        a, b = part[:half], part[half:]
-        keep_ref[k] = jnp.where(low, a, b)
-        give_ref[k] = jnp.where(low, b, a)
+    half = part_ref.shape[1]
+    blocks = near_ref.shape[0] // 2
+    at = pl.ds(half_ref[0] * blocks, blocks)
+    part_ref[0] = dot(near_ref[at, :, :width].reshape(half, width), um[...], 1, 0)
+    part_ref[1] = dot(near_ref[at, :, width:].reshape(half, width), dm[...], 1, 1)
 
 
 def second_kernel(mask_ref, acts_ref, up_ref, down_ref, terms_ref, um, dm):
@@ -171,17 +166,20 @@
     far = far.reshape(1, FARS * rows, 2 * width)
     near = near_swap(jnp.broadcast_to(far, (NEARS,) + far.shape[1:]))
 
-    keep, give = pl.pallas_call(
+    partial_sums = pl.pallas_call(
         first_kernel,
         in_specs=[smem, smem, vmem, vmem, vmem],
-        out_specs=[vmem, vmem],
-        out_shape=[jax.ShapeDtypeStruct((2, half, units), f4)] * 2,
+        out_specs=vmem,
+        out_shape=jax.ShapeDtypeStruct((2, half, units), f4),
         scratch_shapes=scratch,
         compiler_params=params,
         cost_estimate=cost,
         name="partial_sums",
-    )(core.reshape(1), mask, near, up_weight, down_weight)
-    pair = keep + lax.ppermute(give, "core", [(0, 1), (1, 0)])
+    )
+    give = partial_sums((1 - core).reshape(1), mask, near, up_weight, down_weight)
+    got = lax.ppermute(give, "core", [(0, 1), (1, 0)])
+    keep = partial_sums(core.reshape(1), mask, near, up_weight, down_weight)
+    pair = keep + got
     pair = pair.reshape(2, 4, quarter, units).transpose(1, 0, 2, 3)
     sent = pair.astype(bf)
     lost = lax.dynamic_index_in_dim(pair, lax.axis_index(LINE), 0, keepdims=False)

time: 129 us -> 133 us (1.031)
  the two profiles are of different devices: /device:TPU:8 before, /device:TPU:10 now
where the time goes in v7:
time: 133 us; the launch traced here: 132 us
  waiting for transfers between devices  46.9 us (35%)
  blocking collectives  36.1 us (27%)
  starting transfers between devices  29.2 us (22%)
  Pallas kernels  9.66 us (7%)
  local copies, waits for them, and re-layouts  7.78 us (6%)
  other arithmetic  1.41 us (1%)
    all_to_all x1, waiting for transfers between devices, spread(): return lax.all_to_all(copies, axes, split_axis=0, concat_axis=0, tiled=True)  18.7 us
    all_to_all x1, waiting for transfers between devices, swap(): return lax.all_to_all(blocks, axes, split_axis=0, concat_axis=0, tiled=True)  16.5 us
    all_to_all x1, starting transfers between devices, spread(): return lax.all_to_all(copies, axes, split_axis=0, concat_axis=0, tiled=True)  16.3 us
    all_to_all x1, blocking collectives, near_swap(): lax.all_to_all(blocks, AXES, split_axis=0, concat_axis=0, tiled=True, axi...  14.7 us
    all_to_all x1, waiting for transfers between devices, near_swap(): lax.all_to_all(blocks, AXES, split_axis=0, concat_axis=0, tiled=True, axi...  11.7 us
    all_to_all x1, blocking collectives, swap(): return lax.all_to_all(blocks, axes, split_axis=0, concat_axis=0, tiled=True)  9.72 us
    all_to_all x1, blocking collectives, spread(): return lax.all_to_all(copies, axes, split_axis=0, concat_axis=0, tiled=True)  9.58 us
    all_to_all x1, starting transfers between devices, swap(): return lax.all_to_all(blocks, axes, split_axis=0, concat_axis=0, tiled=True)  5.88 us
  transfers between devices with their start and end apart: 4, of which 3 were waited for; matrix products, arithmetic and copies ran while one was open for 1% of the time, Pallas kernels for 5%

profile of v7, /device:TPU:10, one launch (start us, length us, event | category | flops | bytes accessed | tf_op | source)
XLA Modules:
  0.0 131.9 jit_solution(7922342777887248148)
XLA Ops:
  0.6 0.7 pad_maximum_fusion.1
  1.4 0.8 broadcast_in_dim.8
  2.2 16.3 %all-to-all-start = ((bf16[16,4,3072]{2,1,0:T(4,128)(2,1)}), bf16[16,4,3072]{2,1,0:T(4,128)(2,1)S(1)}, u32[]{:S(2)}, u32[]{:S(2)}) async-start(bf16[16,4,3072]{2,1,0:T(4,128)(2,1)} %broadcast_in_dim.8), calls=%async_computation | async-start | bytes 786432 | tf_op jit(solution)/shard_map/all_to_all | solution.py:54
  18.6 0.8 dynamic_slice.5.mask_ref
  19.4 18.7 %all-to-all-done = bf16[16,4,3072]{2,1,0:T(4,128)(2,1)S(1)} async-done(((bf16[16,4,3072]{2,1,0:T(4,128)(2,1)}), bf16[16,4,3072]{2,1,0:T(4,128)(2,1)S(1)}, u32[]{:S(2)}, u32[]{:S(2)}) %all-to-all-start) | async-done | bytes 393248 | tf_op jit(solution)/shard_map/all_to_all | solution.py:54
  38.2 1.3 %broadcast_in_dim.10 = bf16[4,64,3072]{2,1,0:T(8,128)(2,1)} broadcast(bf16[64,3072]{1,0:T(8,128)(2,1)S(1)} %broadcast_in_dim.9), dimensions={1,2} | broadcast | bytes 1966080 | tf_op jit(solution)/shard_map/broadcast_in_dim | solution.py:167
  39.5 5.1 %all-to-all-start.1 = ((bf16[4,64,3072]{2,1,0:T(8,128)(2,1)}), bf16[4,64,3072]{2,1,0:T(8,128)(2,1)S(1)}, u32[]{:S(2)}, u32[]{:S(2)}) async-start(bf16[4,64,3072]{2,1,0:T(8,128)(2,1)} %broadcast_in_dim.10), calls=%async_computation.1 | async-start | bytes 3145728 | tf_op jit(solution)/shard_map/all_to_all | solution.py:47
  44.6 11.7 %all-to-all-done.1.near_ref.saved_ref = bf16[4,64,3072]{2,1,0:T(8,128)(2,1)S(1)} async-done(((bf16[4,64,3072]{2,1,0:T(8,128)(2,1)}), bf16[4,64,3072]{2,1,0:T(8,128)(2,1)S(1)}, u32[]{:S(2)}, u32[]{:S(2)}) %all-to-all-start.1) | async-done | bytes 1572896 | tf_op jit(solution)/shard_map/all_to_all | solution.py:47
  56.3 1.8 %copy-done.2 = bf16[384,1536]{1,0:T(8,128)(2,1)S(1)} copy-done((bf16[384,1536]{1,0:T(8,128)(2,1)S(1)}, bf16[384,1536]{1,0:T(8,128)(2,1)}, u32[]{:S(2)}) %copy-start.2) | copy-done | bytes 1179672
  58.2 1.7 %partial_sums.3 = f32[2,128,384]{2,1,0:T(8,128)S(1)} custom-call(s32[1]{0:T(128)} %bitcast.1.half_ref, s32[12,3]{1,0:T(8,128)S(1)} %dynamic_slice.5.mask_ref, bf16[4,64,3072]{2,1,0:T(8,128)(2,1)S(1)} %all-to-all-done.1.near_ref.saved_ref, bf16[1536,384]{1,0:T(8,128)(2,1)S(1)} %copy-done.1, bf16[384,1536]{1,0:T(8,128)(2,1)S(1)} %copy-done.2), custom_call_target="tpu_custom_call" | custom-call | flops 603979776 | bytes 3932160 | tf_op jit(solution)/shard_map/partial_sums/pallas_call | solution.py:179
  59.8 1.9 %collective-permute-start = (f32[2,128,384]{2,1,0:T(8,128)S(1)}, f32[2,128,384]{2,1,0:T(8,128)S(1)}, u32[]{:S(2)}, u32[]{:S(2)}) collective-permute-start(f32[2,128,384]{2,1,0:T(8,128)S(1)} %partial_sums.3), channel_id=1, source_target_pairs={{0,1},{1,0},{2,3},{3,2},{4,5},{5,4},{6,7},{7,6},{8,9},{9,8},{10,11... | collective-permute-start | bytes 1179656 | tf_op jit(solution)/shard_map/ppermute | solution.py:180
  61.8 1.3 copy-done.3
  63.1 1.7 %partial_sums.2 = f32[2,128,384]{2,1,0:T(8,128)S(1)} custom-call(s32[1]{0:T(128)} %bitcast.half_ref, s32[12,3]{1,0:T(8,128)S(1)} %dynamic_slice.5.mask_ref, bf16[4,64,3072]{2,1,0:T(8,128)(2,1)S(1)} %all-to-all-done.1.near_ref.saved_ref, bf16[1536,384]{1,0:T(8,128)(2,1)S(1)} %copy-done.1, bf16[384,1536]{1,0:T(8,128)(2,1)S(1)} %copy-done.3), custom_call_target="tpu_custom_call" | custom-call | flops 603979776 | bytes 3932160 | tf_op jit(solution)/shard_map/partial_sums/pallas_call | solution.py:181
  64.9 9.7 %all_to_all.30 = bf16[4,2,32,384]{3,2,1,0:T(8,128)(2,1)S(1)} all-to-all(bf16[4,2,32,384]{3,2,1,0:T(8,128)(2,1)S(1)} %bitcast.17), channel_id=1, replica_groups=mesh['zh'=4,'zl'=2,'xh'=2,'xl'=2,'yh'=2,'ylh'=2,'yll'=2,'core'=2] {'yll'..., dimensions={0} | all-to-all | bytes 393216 | tf_op jit(solution)/shard_map/all_to_all | solution.py:58
  74.7 9.6 %all_to_all.31 = bf16[4,2,32,384]{3,2,1,0:T(8,128)(2,1)S(1)} all-to-all(bf16[4,2,32,384]{3,2,1,0:T(8,128)(2,1)S(1)} %broadcast_in_dim.22), channel_id=1, replica_groups=mesh['zh'=4,'zl'=2,'xh'=2,'xl'=2,'yh'=2,'ylh'=2,'yll'=2,'core'=2] {'yll'..., dimensions={0} | all-to-all | bytes 393216 | tf_op jit(solution)/shard_map/all_to_all | solution.py:54
  84.3 2.1 %all_gather.3 = bf16[2,256,384]{2,1,0:T(8,128)(2,1)S(1)} all-gather(bf16[1,256,384]{2,1,0:T(8,128)(2,1)S(1)} %bitcast.18), channel_id=1, replica_groups=mesh['zh'=4,'zl'=2,'xh'=2,'xl'=2,'yh'=2,'ylh'=2,'yll'=2,'core'=2] {'core'}, dimensions={0}, use_global_device_ids=true | all-gather | bytes 589824 | tf_op jit(solution)/shard_map/all_gather | solution.py:192
  86.4 1.7 %output_terms.1 = bf16[4,64,3072]{2,1,0:T(8,128)(2,1)S(1)} custom-call(s32[12,3]{1,0:T(8,128)S(1)} %dynamic_slice.5.mask_ref, bf16[8,2,32,384]{3,2,1,0:T(8,128)(2,1)S(1)} %bitcast.13, bf16[1536,384]{1,0:T(8,128)(2,1)S(1)} %copy-done.1, bf16[384,1536]{1,0:T(8,128)(2,1)S(1)} %copy-done.4), custom_call_target="tpu_custom_call" | custom-call | flops 603979776 | bytes 3932160 | tf_op jit(solution)/shard_map/output_terms/pallas_call | solution.py:194
  88.2 14.7 %all_to_all.32 = bf16[4,64,3072]{2,1,0:T(8,128)(2,1)S(1)} all-to-all(bf16[4,64,3072]{2,1,0:T(8,128)(2,1)S(1)} %output_terms.1), channel_id=1, replica_groups={{0,64,16,80},{32,96,48,112},{128,192,144,208},{160,224,176,240},{256,32..., dimensions={0} | all-to-all | bytes 3145728 | tf_op jit(solution)/shard_map/all_to_all | solution.py:47
  102.9 0.3 reduce_sum.34
  103.2 0.9 reshape.51
  104.1 5.9 %all-to-all-start.5 = ((bf16[16,4,3072]{2,1,0:T(4,128)(2,1)}), bf16[16,4,3072]{2,1,0:T(4,128)(2,1)S(1)}, u32[]{:S(2)}, u32[]{:S(2)}) async-start(bf16[16,4,3072]{2,1,0:T(4,128)(2,1)} %reshape.51), calls=%async_computation.5 | async-start | bytes 786432 | tf_op jit(solution)/shard_map/all_to_all | solution.py:58
  110.0 4.6 %weight_grads.1 = (bf16[1536,384]{1,0:T(8,128)(2,1)}, bf16[384,1536]{1,0:T(8,128)(2,1)}) custom-call(s32[12,3]{1,0:T(8,128)} %copy-done.6, bf16[8,2,32,384]{3,2,1,0:T(8,128)(2,1)} %bitcast.14, bf16[4,64,3072]{2,1,0:T(8,128)(2,1)} %copy-done), custom_call_target="tpu_custom_call" | custom-call | flops 603979776 | bytes 3932160 | tf_op jit(solution)/shard_map/weight_grads/pallas_call | solution.py:211
  114.6 16.5 %all-to-all-done.5 = bf16[16,4,3072]{2,1,0:T(4,128)(2,1)S(1)} async-done(((bf16[16,4,3072]{2,1,0:T(4,128)(2,1)}), bf16[16,4,3072]{2,1,0:T(4,128)(2,1)S(1)}, u32[]{:S(2)}, u32[]{:S(2)}) %all-to-all-start.5) | async-done | bytes 393248 | tf_op jit(solution)/shard_map/all_to_all | solution.py:58
  131.3 0.6 fusion.8
  (23 shorter events, 0.5 us)
Async XLA Ops:
  2.2 35.9 %all-to-all-start = ((bf16[16,4,3072]{2,1,0:T(4,128)(2,1)}), bf16[16,4,3072]{2,1,0:T(4,128)(2,1)S(1)}, u32[]{:S(2)}, u32[]{:S(2)}) async-start(bf16[16,4,3072]{2,1,0:T(4,128)(2,1)} %broadcast_in_dim.8), calls=%async_computation | async-start | bytes 786432 | tf_op jit(solution)/shard_map/all_to_all | solution.py:54
  19.4 67.0 %copy-start.6 = (s32[12,3]{1,0:T(8,128)}, s32[12,3]{1,0:T(8,128)S(1)}, u32[]{:S(2)}) copy-start(s32[12,3]{1,0:T(8,128)S(1)} %dynamic_slice.5.mask_ref) | copy-start | bytes 436
  39.5 16.8 %copy-start.1 = (bf16[1536,384]{1,0:T(8,128)(2,1)S(1)}, bf16[1536,384]{1,0:T(8,128)(2,1)}, u32[]{:S(2)}) copy-start(bf16[1536,384]{1,0:T(8,128)(2,1)} %up_ref.5) | copy-start | bytes 3538948
  39.5 16.8 %all-to-all-start.1 = ((bf16[4,64,3072]{2,1,0:T(8,128)(2,1)}), bf16[4,64,3072]{2,1,0:T(8,128)(2,1)S(1)}, u32[]{:S(2)}, u32[]{:S(2)}) async-start(bf16[4,64,3072]{2,1,0:T(8,128)(2,1)} %broadcast_in_dim.10), calls=%async_computation.1 | async-start | bytes 3145728 | tf_op jit(solution)/shard_map/all_to_all | solution.py:47
  56.3 5.4 %copy-start = (bf16[4,64,3072]{2,1,0:T(8,128)(2,1)}, bf16[4,64,3072]{2,1,0:T(8,128)(2,1)S(1)}, u32[]{:S(2)}) copy-start(bf16[4,64,3072]{2,1,0:T(8,128)(2,1)S(1)} %all-to-all-done.1.near_ref.saved_ref) | copy-start | bytes 4718596
  56.3 1.8 %copy-start.2 = (bf16[384,1536]{1,0:T(8,128)(2,1)S(1)}, bf16[384,1536]{1,0:T(8,128)(2,1)}, u32[]{:S(2)}) copy-start(bf16[384,1536]{1,0:T(8,128)(2,1)} %down_ref.5) | copy-start | bytes 3538948
  59.8 4.9 %collective-permute-start = (f32[2,128,384]{2,1,0:T(8,128)S(1)}, f32[2,128,384]{2,1,0:T(8,128)S(1)}, u32[]{:S(2)}, u32[]{:S(2)}) collective-permute-start(f32[2,128,384]{2,1,0:T(8,128)S(1)} %partial_sums.3), channel_id=1, source_target_pairs={{0,1},{1,0},{2,3},{3,2},{4,5},{5,4},{6,7},{7,6},{8,9},{9,8},{10,11... | collective-permute-start | bytes 1179656 | tf_op jit(solution)/shard_map/ppermute | solution.py:180
  61.8 1.3 copy-start.3
  64.8 21.6 %copy-start.4 = (bf16[384,1536]{1,0:T(8,128)(2,1)S(1)}, bf16[384,1536]{1,0:T(8,128)(2,1)}, u32[]{:S(2)}) copy-start(bf16[384,1536]{1,0:T(8,128)(2,1)} %down_ref.5) | copy-start | bytes 3538948
  86.4 1.8 %copy-start.5 = (bf16[2,256,384]{2,1,0:T(8,128)(2,1)}, bf16[2,256,384]{2,1,0:T(8,128)(2,1)S(1)}, u32[]{:S(2)}) copy-start(bf16[2,256,384]{2,1,0:T(8,128)(2,1)S(1)} %all_gather.3) | copy-start | bytes 1179652
  104.1 26.9 %all-to-all-start.5 = ((bf16[16,4,3072]{2,1,0:T(4,128)(2,1)}), bf16[16,4,3072]{2,1,0:T(4,128)(2,1)S(1)}, u32[]{:S(2)}, u32[]{:S(2)}) async-start(bf16[16,4,3072]{2,1,0:T(4,128)(2,1)} %reshape.51), calls=%async_computation.5 | async-start | bytes 786432 | tf_op jit(solution)/shard_map/all_to_all | solution.py:58
